TPU v7x, 256 devices: a whole 4x4x8 slice. The times are simulated.
256 devices in a mesh: pre: 16 (over z, core), grp: 4 (over y), kv: 4 (over x).
Axes of the slice: x: 4, y: 4, z: 8, core: 2. Of those that a mesh axis runs over, the one named last changes fastest.
Arguments:
- prefill_kv: bfloat16 [1024, 2, 8, 64, 128], P(('pre', 'grp'), None, 'kv'), may hold values from -6 to 6
- page_match: int32 [64, 64, 1], P(('pre', 'grp')), may hold values from 0 to 15
- queries: bfloat16 [512, 4, 128, 128], P(('pre', 'grp'), None, 'kv'), may hold values from -192 to 192
- new_kv: bfloat16 [512, 4, 2, 8, 128], P(('pre', 'grp'), None, None, 'kv'), may hold values from -6 to 6
- slot_request: int32 [128, 4], P('pre', 'grp'), may hold values from 0 to 511, as said below
- page_table: int32 [128, 4, 32], P('pre', 'grp'), may hold values from 0 to 63
- context_len: int32 [128, 4], P('pre', 'grp'), may hold values from 1 to 2048, as said below
- out_weight: bfloat16 [16384, 16384], P('kv', 'pre'), may hold values from -0.1875 to 0.1875
Outputs:
- decoded: bfloat16 [128, 4, 4, 16384], P(None, 'grp', None, ('pre', 'kv'))
Inputs may be any that keep to these rules, and one draw needn't show every extreme that they name: `slot_request`: every request is served by exactly one slot. Requests r with the same r // 2 are served by one decode device, and every decode device serves exactly 2 requests of a source device s (requests s * 8 .. (s + 1) * 8 - 1) or none. `context_len`: some slot's context is exactly 2048 positions long.
All inputs are finite; a program needn't handle non-finite values.
Results may differ from a plain program's by a relative error of at most 0.0052.
Values may be sent and summed in bfloat16 or wider, within the bound.
A program may use at most 128 MiB of HBM per device.

v0:
```python
import jax
import jax.numpy as jnp
from jax import lax
from jax.sharding import PartitionSpec as P

HD = 128
PAGE = 64
STEPS = 4
MAXP = 32


NEG_FILL = -1e30


def body(
    prefill_kv, page_match, queries, new_kv, slot_request, page_table, context_len, out_weight
):
    shards = page_match.shape[1]
    per_cap = page_match.shape[2]
    page_shape = prefill_kv.shape[1:]
    kv_local = prefill_kv.shape[2]
    outgoing = jnp.take(prefill_kv, page_match[0].reshape(-1), axis=0)
    sectioned = outgoing.reshape((shards, per_cap) + page_shape)
    arrived = lax.all_to_all(sectioned, ("pre", "grp"), split_axis=0, concat_axis=0, tiled=True)
    page_pool = arrived.reshape((shards * per_cap,) + page_shape)
    local_slots = queries.shape[0]
    flat_q = queries.reshape(local_slots, -1)
    flat_new = new_kv.reshape(local_slots, -1)
    requests = slot_request.reshape(-1)
    wanted = requests.shape[0]
    piece_q = lax.all_gather(flat_q, ("pre", "grp"), axis=0, tiled=True)
    piece_new = lax.all_gather(flat_new, ("pre", "grp"), axis=0, tiled=True)
    piece_count = piece_q.shape[0]
    match_rows = (requests[:, None] == jnp.arange(piece_count, dtype=jnp.int32)[None, :]).astype(
        jnp.bfloat16
    )
    picked_q = jnp.dot(match_rows, piece_q, preferred_element_type=jnp.float32)
    picked_new = jnp.dot(match_rows, piece_new, preferred_element_type=jnp.float32)
    q_heads = queries.shape[2]
    heads_per = q_heads // kv_local
    rows_q = STEPS * heads_per
    chosen_q = picked_q.astype(jnp.bfloat16).reshape(wanted, STEPS, kv_local, heads_per, HD)
    chosen_q = chosen_q.transpose(0, 2, 1, 3, 4).reshape(wanted, kv_local, rows_q, HD)
    chosen_new = picked_new.astype(jnp.bfloat16).reshape(wanted, STEPS, 2, kv_local, HD)
    scale_qk = 1.0 / HD**0.5
    tables = page_table.reshape(wanted, -1)
    lengths = context_len.reshape(-1)
    new_scores = (
        jnp.einsum(
            "rhqd,ruhd->rhqu", chosen_q, chosen_new[:, :, 0], preferred_element_type=jnp.float32
        )
        * scale_qk
    )
    step_rows = jnp.arange(rows_q, dtype=jnp.int32) // heads_per
    new_valid = jnp.arange(STEPS, dtype=jnp.int32)[None, :] <= step_rows[:, None]
    new_scores = jnp.where(new_valid[None, None], new_scores, NEG_FILL)
    new_top = jnp.max(new_scores, axis=-1)
    fetched = page_pool[tables]
    scores = jnp.einsum(
        "rhqd,rphkd->rhqpk", chosen_q, fetched[:, :, 0], preferred_element_type=jnp.float32
    )
    scores = scores.reshape(wanted, kv_local, rows_q, MAXP * PAGE) * scale_qk
    positions = jnp.arange(MAXP * PAGE, dtype=jnp.int32)
    in_length = positions[None, :] < lengths[:, None]
    scores = jnp.where(in_length[:, None, None, :], scores, NEG_FILL)
    highest = jnp.maximum(jnp.max(scores, axis=-1), new_top)
    weights = jnp.where(in_length[:, None, None, :], jnp.exp(scores - highest[..., None]), 0.0)
    totals = jnp.sum(weights, axis=-1)
    rounded = weights.astype(jnp.bfloat16).reshape(wanted, kv_local, rows_q, MAXP, PAGE)
    weighted = jnp.einsum(
        "rhqpk,rphkd->rhqd", rounded, fetched[:, :, 1], preferred_element_type=jnp.float32
    )
    new_w = jnp.where(new_valid[None, None], jnp.exp(new_scores - highest[..., None]), 0.0)
    totals = totals + jnp.sum(new_w, axis=-1)
    weighted = weighted + jnp.einsum(
        "rhqu,ruhd->rhqd",
        new_w.astype(jnp.bfloat16),
        chosen_new[:, :, 1],
        preferred_element_type=jnp.float32,
    )
    attended = (weighted / totals[..., None]).astype(jnp.bfloat16)
    attended = (
        attended.reshape(wanted, kv_local, STEPS, heads_per, HD)
        .transpose(0, 2, 1, 3, 4)
        .reshape(wanted, 1, STEPS, -1)
    )
    columns = out_weight.shape[1]
    shard_rows = lax.all_gather(attended, "pre", axis=0, tiled=True)
    piece_count = shard_rows.shape[0]
    product = jnp.dot(
        shard_rows.reshape(-1, shard_rows.shape[-1]), out_weight, preferred_element_type=jnp.float32
    )
    partial_value = product.reshape(piece_count, 1, STEPS, columns)
    summed = lax.psum_scatter(partial_value, "kv", scatter_dimension=3, tiled=True)
    return summed.astype(jnp.bfloat16)


def solution(mesh):
    in_specs = (
        P(("pre", "grp"), None, "kv", None, None),
        P(("pre", "grp"), None, None),
        P(("pre", "grp"), None, "kv", None),
        P(("pre", "grp"), None, None, "kv", None),
        P("pre", "grp"),
        P("pre", "grp", None),
        P("pre", "grp"),
        P("kv", "pre"),
    )
    out_specs = P(None, "grp", None, ("pre", "kv"))
    return jax.shard_map(body, mesh=mesh, in_specs=in_specs, out_specs=out_specs, check_vma=False)
```

profile of v0, /device:TPU:1, one launch (start us, length us, event | category | flops | bytes accessed | tf_op | source)
XLA Modules:
  0.0 328.6 jit_solution(8427909927913889505)
XLA Ops:
  6.5 1.5 reshape.182
  8.0 0.0 all-gather.6.cloned.1.call-update
  8.0 0.0 all-gather.4.cloned.1.call-start
  8.1 1.8 copy.54
  9.9 0.0 all-gather.4.cloned.1.call-update
  9.9 0.7 fusion.32
  10.6 3.0 gather_fusion
  13.7 4.6 %bitcast_select_fusion = bf16[64,1,2,2,64,128]{5,4,3,2,1,0:T(8,128)(2,1)} fusion(bf16[64,2,2,64,128]{4,3,2,1,0:T(8,128)(2,1)} %gather_fusion, pred[64]{0:T(512)(128)(4,1)S(1)} %compare_and_fusion), kind=kLoop, calls=%fused_computation.19 | loop fusion | flops 2097152 | bytes 8388672 | tf_op jit(solution)/shard_map/jit(_take)/select_n | solution.py:22
  18.3 13.3 %all-to-all-start = ((bf16[64,1,2,2,64,128]{5,4,3,2,1,0:T(8,128)(2,1)}), bf16[64,1,2,2,64,128]{5,4,3,2,1,0:T(8,128)(2,1)}, u32[]{:S(2)}, u32[]{:S(2)}) async-start(bf16[64,1,2,2,64,128]{5,4,3,2,1,0:T(8,128)(2,1)} %bitcast_select_fusion), calls=%async_computation | async-start | bytes 8388608 | tf_op jit(solution)/shard_map/all_to_all | solution.py:24
  31.6 0.0 all-gather.8.cloned.1.call-start
  31.7 0.1 reshape.197
  31.8 0.1 broadcast_compare_fusion
  31.9 72.6 %all-gather.6.cloned.1.call-done = bf16[512,2048]{1,0:T(8,128)(2,1)} async-done(((bf16[8,2048]{1,0:T(8,128)(2,1)}), bf16[512,2048]{1,0:T(8,128)(2,1)}) %all-gather.6.cloned.1.call-update) | async-done | bytes 2097168 | tf_op jit(solution)/shard_map/all_gather | solution.py:32
  104.5 2.0 convolution_convert_fusion.1
  106.5 28.5 %all-to-all-done = bf16[64,1,2,2,64,128]{5,4,3,2,1,0:T(8,128)(2,1)} async-done(((bf16[64,1,2,2,64,128]{5,4,3,2,1,0:T(8,128)(2,1)}), bf16[64,1,2,2,64,128]{5,4,3,2,1,0:T(8,128)(2,1)}, u32[]{:S(2)}, u32[]{:S(2)}) %all-to-all-start) | async-done | bytes 4194336 | tf_op jit(solution)/shard_map/all_to_all | solution.py:24
  135.1 12.0 %gather_fusion.1 = bf16[256,2,2,64,128]{4,3,2,1,0:T(8,128)(2,1)} fusion(bf16[64,2,2,64,128]{4,3,2,1,0:T(8,128)(2,1)} %bitcast.11, s32[1024]{0:T(1024)S(1)} %pad_clamp_fusion), kind=kCustom, calls=%fused_computation.1 | custom fusion | bytes 33555456 | tf_op jit(solution)/shard_map/gather | solution.py:58
  147.0 14.9 %fusion.37 = (bf16[8,32,1,2,64,128]{5,4,3,2,1,0:T(8,128)(2,1)}, bf16[8,32,1,2,64,128]{5,4,3,2,1,0:T(8,128)(2,1)}) fusion(bf16[8,32,2,2,64,128]{5,4,3,2,1,0:T(8,128)(2,1)} %bitcast.70), kind=kLoop, calls=%fused_computation.58 | loop fusion | bytes 33554432 | tf_op jit(solution)/shard_map/slice | solution.py:60
  161.9 47.2 %all-gather.4.cloned.1.call-done = bf16[512,16384]{1,0:T(8,128)(2,1)} async-done(((bf16[8,16384]{1,0:T(8,128)(2,1)}), bf16[512,16384]{1,0:T(8,128)(2,1)}) %all-gather.4.cloned.1.call-update) | async-done | bytes 16777232 | tf_op jit(solution)/shard_map/all_gather | solution.py:31
  209.2 8.2 %convolution_convert_fusion = bf16[8,16384]{1,0:T(8,128)(2,1)S(1)} fusion(bf16[512,16384]{1,0:T(8,128)(2,1)} %all-gather.4.cloned.1.call-done, s32[8]{0:T(128)S(1)} %bitcast.82), kind=kOutput, calls=%fused_computation.2 | convolution fusion | flops 134352896 | bytes 17039392 | tf_op jit(solution)/shard_map/dot_general | solution.py:37
  217.4 0.1 copy.23
  217.5 5.7 %fusion = (f32[8,2,64]{2,1,0:T(2,128)S(1)}, f32[8,2,64,32,64]{2,4,3,1,0:T(8,128)S(1)}) fusion(pred[8,32,64]{2,1,0:T(8,128)(4,1)S(1)} %broadcast_compare_fusion, bf16[8,2,64,128,1]{3,2,4,1,0:T(8,128)(2,1)S(1)} %bitcast.77, bf16[8,32,1,2,64,128]{5,4,3,2,1,0:T(8,128)(2,1)S(1)} %copy-done.2), kind=kOutput, calls=%fused_computation.5 | convolution fusion | flops 543161344 | bytes 17059840 | tf_op jit(solution)/shard_map/rhqd,rphkd->rhqpk/dot_general | solution.py:59
  223.2 0.3 fusion.39
  223.5 5.6 %fusion.1 = f32[8,2,64]{2,1,0:T(2,128)S(1)} fusion(f32[8,2,64,32,64]{2,4,3,1,0:T(8,128)S(1)} %get-tuple-element.10, f32[8,2,64]{2,1,0:T(2,128)S(1)} %max.7, pred[8,32,64]{2,1,0:T(8,128)(4,1)S(1)} %broadcast_compare_fusion), kind=kLoop, calls=%fused_computation.6 | loop fusion | flops 10484736 | bytes 8413184 | tf_op jit(solution)/shard_map/reduce_sum | solution.py:68
  229.2 9.2 %fusion.19 = f32[8,2,64,128]{3,2,1,0:T(8,128)S(1)} fusion(bf16[8,32,1,2,64,128]{5,4,3,2,1,0:T(8,128)(2,1)S(1)} %bitcast.72, f32[8,2,64,32,64]{2,4,3,1,0:T(8,128)S(1)} %get-tuple-element.10, f32[8,2,64]{2,1,0:T(2,128)S(1)} %max.7, pred[8,32,64]{2,1,0:T(8,128)(4,1)S(1)} %broadcast_compare_fusion), kind=kOutput, calls=%fused_computation.24 | convolution fusion | flops 547356672 | bytes 17321984 | tf_op jit(solution)/shard_map/rhqpk,rphkd->rhqd/dot_general | solution.py:70
  238.4 0.3 fusion.22
  238.8 0.9 copy.29
  239.7 0.2 reduce-scatter.2.cloned.1.call-start
  239.9 39.0 %all-gather.8.cloned.1.call-done = bf16[128,1,4,4096]{3,0,2,1:T(8,128)(2,1)} async-done(((bf16[8,1,4,4096]{3,0,2,1:T(8,128)(2,1)}), bf16[128,1,4,4096]{3,0,2,1:T(8,128)(2,1)}) %all-gather.8.cloned.1.call-update) | async-done | bytes 4194320 | tf_op jit(solution)/shard_map/all_gather | solution.py:88
  278.9 10.6 %fusion.13 = f32[128,1,4,1024]{3,0,2,1:T(8,128)} fusion(bf16[4096,1024]{1,0:T(8,128)(2,1)} %param.15, bf16[128,1,4,4096]{3,0,2,1:T(8,128)(2,1)} %all-gather.8.cloned.1.call-done), kind=kOutput, calls=%fused_computation.21 | convolution fusion | flops 4294967296 | bytes 14680064 | tf_op jit(solution)/shard_map/dot_general | solution.py:90
  289.5 30.6 %reduce-scatter.2.cloned.1.call-done = f32[128,1,4,256]{3,0,2,1:T(8,128)} async-done(((f32[128,1,4,1024]{3,0,2,1:T(8,128)}), f32[128,1,4,256]{3,0,2,1:T(8,128)}) %reduce-scatter.2.cloned.1.call-update) | async-done | bytes 524304 | tf_op jit(solution)/shard_map/reduce_scatter | solution.py:94
  320.1 1.1 convert_element_type.25
  321.1 0.9 copy.30
  (33 shorter events, 0.2 us)
Async XLA Ops:
  6.5 4.1 %copy-start = (bf16[16,2,2,64,128]{4,3,2,1,0:T(8,128)(2,1)S(1)}, bf16[16,2,2,64,128]{4,3,2,1,0:T(8,128)(2,1)}, u32[]{:S(2)}) copy-start(bf16[16,2,2,64,128]{4,3,2,1,0:T(8,128)(2,1)} %param.8) | copy-start | bytes 3145732
  6.5 7.1 %copy-start.6 = (s32[1,64,1]{1,2,0:T(1,128)S(1)}, s32[1,64,1]{1,2,0:T(1,128)}, u32[]{:S(2)}) copy-start(s32[1,64,1]{1,2,0:T(1,128)} %param.9) | copy-start | bytes 772
  6.5 98.0 %all-gather.6.cloned.1.call-start = ((), (), s32[]{:S(2)}) async-start(), calls=%async_computation.3 | async-start | bytes 2129920 | tf_op jit(solution)/shard_map/all_gather | solution.py:32
  8.0 201.1 %all-gather.4.cloned.1.call-start = ((), (), s32[]{:S(2)}) async-start(), calls=%async_computation.2 | async-start | bytes 17039360 | tf_op jit(solution)/shard_map/all_gather | solution.py:31
  13.7 18.0 %copy-start.4 = (s32[8,1,32]{2,1,0:T(1,128)S(1)}, s32[8,1,32]{2,1,0:T(1,128)}, u32[]{:S(2)}) copy-start(s32[8,1,32]{2,1,0:T(1,128)} %param.13) | copy-start | bytes 3076
  13.7 18.2 %copy-start.5 = (s32[8,1]{0,1:T(1,128)S(1)}, s32[8,1]{0,1:T(1,128)}, u32[]{:S(2)}) copy-start(s32[8,1]{0,1:T(1,128)} %param.14) | copy-start | bytes 100
  13.7 90.8 %copy-start.3 = (s32[8,1]{0,1:T(1,128)S(1)}, s32[8,1]{0,1:T(1,128)}, u32[]{:S(2)}) copy-start(s32[8,1]{0,1:T(1,128)} %param.12) | copy-start | bytes 100
  18.3 116.8 %all-to-all-start = ((bf16[64,1,2,2,64,128]{5,4,3,2,1,0:T(8,128)(2,1)}), bf16[64,1,2,2,64,128]{5,4,3,2,1,0:T(8,128)(2,1)}, u32[]{:S(2)}, u32[]{:S(2)}) async-start(bf16[64,1,2,2,64,128]{5,4,3,2,1,0:T(8,128)(2,1)} %bitcast_select_fusion), calls=%async_computation | async-start | bytes 8388608 | tf_op jit(solution)/shard_map/all_to_all | solution.py:24
  31.6 247.3 %all-gather.8.cloned.1.call-start = ((), (), s32[]{:S(2)}) async-start(), calls=%async_computation.4 | async-start | bytes 4456448 | tf_op jit(solution)/shard_map/all_gather | solution.py:88
  209.2 8.3 %copy-start.2 = (bf16[8,32,1,2,64,128]{5,4,3,2,1,0:T(8,128)(2,1)S(1)}, bf16[8,32,1,2,64,128]{5,4,3,2,1,0:T(8,128)(2,1)}, u32[]{:S(2)}) copy-start(bf16[8,32,1,2,64,128]{5,4,3,2,1,0:T(8,128)(2,1)} %get-tuple-element.5) | copy-start | bytes 25165828
  209.2 20.0 %slice-start = ((s8[8388608]{0:T(1024)(128)(4,1)}), s8[4194304]{0:T(1024)(128)(4,1)S(1)}, s32[]{:S(2)}) async-start(s8[8388608]{0:T(1024)(128)(4,1)} %bitcast.71), calls=%async_computation.6 | async-start | bytes 8388608
  217.5 11.7 %slice-start.1 = ((s8[8388608]{0:T(1024)(128)(4,1)}), s8[4194304]{0:T(1024)(128)(4,1)S(1)}, s32[]{:S(2)}) async-start(s8[8388608]{0:T(1024)(128)(4,1)} %bitcast.71), calls=%async_computation.7 | async-start | bytes 8388608
  239.7 80.4 %reduce-scatter.2.cloned.1.call-start = ((), (), s32[]{:S(2)}) async-start(), calls=%async_computation.5 | async-start | bytes 2621440 | tf_op jit(solution)/shard_map/reduce_scatter | solution.py:94
  278.9 43.1 %copy-start.1 = (bf16[16,2,2,64,128]{4,3,2,1,0:T(8,128)(2,1)S(1)}, bf16[16,2,2,64,128]{4,3,2,1,0:T(8,128)(2,1)}, u32[]{:S(2)}) copy-start(bf16[16,2,2,64,128]{4,3,2,1,0:T(8,128)(2,1)} %param.8) | copy-start | bytes 3145732
Sparse Core Ops, SparseCore 0:
  10.1 94.3 all-gather.5
  107.3 101.8 all-gather.3
  239.8 39.0 all-gather.7
  289.6 30.4 reduce-scatter.1
where the time goes:
time: 329 us
  waiting for transfers between devices  218 us (66%)
  matrix products  36.3 us (11%)
  local copies, waits for them, and re-layouts  35.2 us (11%)
  starting transfers between devices  13.7 us (4%)
  between operations  13.3 us (4%)
  other arithmetic  12.1 us (4%)
    all_gather x1, waiting for transfers between devices, body(): piece_new = lax.all_gather(flat_new, ('pre', 'grp'), axis=0, tiled=True)  72.6 us
    all_gather x1, waiting for transfers between devices, body(): piece_q = lax.all_gather(flat_q, ('pre', 'grp'), axis=0, tiled=True)  47.2 us
    all_gather x1, waiting for transfers between devices, body(): shard_rows = lax.all_gather(attended, 'pre', axis=0, tiled=True)  39 us
    reduce_scatter x1, waiting for transfers between devices, body(): lax.psum_scatter(partial_value, 'kv', scatter_dimension=3, tiled=True)  30.6 us
    all_to_all x1, waiting for transfers between devices, body(): lax.all_to_all(sectioned, ('pre', 'grp'), split_axis=0, concat_axis=0, ti...  28.5 us
    slice x1, local copies, waits for them, and re-layouts, body(): fetched[:, :, 0]  14.9 us
    all_to_all x1, starting transfers between devices, body(): lax.all_to_all(sectioned, ('pre', 'grp'), split_axis=0, concat_axis=0, ti...  13.3 us
    gather x1, local copies, waits for them, and re-layouts, body(): fetched = page_pool[tables]  12 us
  transfers between devices with their start and end apart: 5, of which 5 were waited for; matrix products, arithmetic and copies ran while one was open for 12% of the time, Pallas kernels for 0%

commit v1 on v0

v1 whole, which is shorter than its diff:
```python
import functools

import jax
import jax.numpy as jnp
from jax import lax
from jax.experimental import pallas as pl
from jax.experimental.pallas import tpu as pltpu
from jax.sharding import PartitionSpec as P

MESH = pl.DeviceIdType.MESH
HD = 128
PAGE = 64
STEPS = 4
MAXP = 32
NZ = 8
NM = 8
LOG2E = 1.4426950408889634
SCALE = LOG2E / HD**0.5
DEAD = -1e30
MIB = 1 << 20
NG = 4
NT = (((1,), (1,)), ((), ()))


def here():
    p = lax.axis_index("pre")
    return p // 2, p % 2, lax.axis_index("grp")


def dev(z, c, y):
    return {"pre": z * 2 + c, "grp": y}


def dev_zm(z, m):
    return dev(z, m // 4, m % 4)


def wrap(a, n):
    return lax.rem(a + 2 * n, n)


def remote(src, dst, ssem, rsem, device):
    return pltpu.make_async_remote_copy(
        src_ref=src, dst_ref=dst, send_sem=ssem, recv_sem=rsem, device_id=device, device_id_type=MESH
    )


def split3(x):
    hi = x.astype(jnp.bfloat16).astype(jnp.float32)
    mid = (x - hi).astype(jnp.bfloat16).astype(jnp.float32)
    return hi, mid, x - hi - mid


def merge(a, b):
    acc_a, m_a, l_a = a
    acc_b, m_b, l_b = b
    top = jnp.maximum(m_a, m_b)
    fa = jnp.exp2(m_a - top)
    fb = jnp.exp2(m_b - top)
    return acc_a * fa + acc_b * fb, top, l_a * fa + l_b * fb


def attend_kernel(
    qx, ti, mm, pg, out,
    i1, sb, sbn, qg, ng, tig, mmv, mms, pgs, kd, vt, bi, rs_out, rs_in,
    p1s, p1r, tis, tir, mss, msr, loc, ys, yr, ys2, yr2, cs, cr, p2s, p2r, p3s, p3r, as_, ar, rss, rsr,
):
    z, c, y = here()
    me_m = c * 4 + y

    bar = pltpu.get_barrier_semaphore()

    def greet(k, carry):
        j = lax.rem(z * 8 + me_m + k, 64)
        pl.semaphore_signal(bar, inc=1, device_id=dev_zm(j // 8, j % 8), device_id_type=MESH)
        return carry

    lax.fori_loop(1, 64, greet, 0)

    own_pages = pltpu.make_async_copy(pg, pgs.at[me_m], loc.at[0])
    own_pages.start()
    i1[z, me_m] = qx[z, me_m]
    tig[z] = ti[...]
    mmv[me_m] = mm[...]
    pl.semaphore_wait(bar, 63)

    def spread(kz, km):
        zj = lax.rem(z + kz, 8)
        mj = lax.rem(me_m + km, 8)
        k = kz * 8 + km
        return remote(qx.at[zj, mj], i1.at[z, me_m], p1s.at[k], p1r.at[k], dev_zm(zj, mj))

    def start_spread(kz, lo):
        def one(km, carry):
            spread(kz, km).start()
            return carry

        lax.fori_loop(lo, 8, one, 0)

    for kz in (4, 3, 5, 2, 6, 1, 7):
        start_spread(kz, 0)
    start_spread(0, 1)

    def table_copy(kz):
        zj = lax.rem(z + kz, 8)
        return remote(ti, tig.at[z], tis.at[kz], tir.at[kz], dev(zj, c, y))

    def match_copy(km):
        mj = lax.rem(me_m + km, 8)
        return remote(mm, mmv.at[me_m], mss.at[km], msr.at[km], dev_zm(z, mj))

    def start_small(k, carry):
        table_copy(k).start()
        match_copy(k).start()
        return carry

    lax.fori_loop(1, 8, start_small, 0)

    y_up, y_dn = wrap(y + 1, 4), wrap(y - 1, 4)

    def m_of(cc, yy):
        return cc * 4 + wrap(yy, 4)

    def quarter(m, q):
        return pgs.at[m, pl.ds(4 * q, 4)]

    def y_copy(direction, q):
        target = dev(z, c, y_up if direction == 0 else y_dn)
        return remote(pg.at[pl.ds(4 * q, 4)], quarter(me_m, q), ys.at[direction, q], yr.at[direction, q], target)

    def y_far(direction, q):
        target = dev(z, c, y_up if direction == 0 else y_dn)
        m = m_of(c, y - 1 if direction == 0 else y + 1)
        return remote(quarter(m, q), quarter(m, q), ys2.at[q], yr2.at[q], target)

    def core_copy(dy, q):
        m = m_of(c, y + dy)
        src = pg.at[pl.ds(4 * q, 4)] if dy == 0 else quarter(m, q)
        return remote(src, quarter(m, q), cs.at[dy, q], cr.at[dy, q], dev(z, 1 - c, y))

    order = ((0, 1, 2, 3), (2, 3, 0, 1))
    for n in range(4):
        for direction in range(2):
            y_copy(direction, order[direction][n]).start()
    for q in range(4):
        core_copy(0, q).start()

    def wait_spread_kz(kz, lo):
        def one(km, carry):
            spread(kz, km).wait_recv()
            return carry

        lax.fori_loop(lo, 8, one, 0)

    wait_spread_kz(0, 1)
    for kz in (1, 7, 2, 6, 3, 5, 4):
        wait_spread_kz(kz, 0)

    arrived = i1[...].astype(jnp.float32).reshape(64, 32, 128)
    table = jnp.concatenate(
        [arrived[:, 0:8].reshape(512, 128), arrived[:, 8:16].reshape(512, 128), arrived[:, 16:24].reshape(512, 128)],
        axis=1,
    ).astype(jnp.bfloat16)
    ids = arrived[:, 24:32].reshape(512, 128)
    request = (ids[:, 0:1] * 8.0 + ids[:, 64:65]).astype(jnp.int32)
    hot = (request == lax.broadcasted_iota(jnp.int32, (512, 512), 1)).astype(jnp.float32).astype(jnp.bfloat16)
    moved = jnp.dot(hot, table, preferred_element_type=jnp.float32).reshape(8, 8, 8, 384)
    for m in range(8):
        for d in range(8):
            rows = moved[d, m]
            sb[m, d] = jnp.concatenate([rows[:, 0:128], rows[:, 128:256]], axis=0).astype(jnp.bfloat16)
        for d in range(0, 8, 2):
            pair = jnp.concatenate([moved[d, m][:, 256:384], moved[d + 1, m][:, 256:384]], axis=0)
            sbn[m, d // 2] = pair.astype(jnp.bfloat16)

    def to_slots(km):
        mj = lax.rem(me_m + km, 8)
        return (
            remote(sb.at[mj], qg.at[z, me_m], p2s.at[km], p2r.at[km], dev_zm(z, mj)),
            remote(sbn.at[mj], ng.at[me_m], p3s.at[km], p3r.at[km], dev_zm(z, mj)),
        )

    def start_slots(km, carry):
        for copy in to_slots(km):
            copy.start()
        return carry

    lax.fori_loop(1, 8, start_slots, 0)
    qg[z, me_m] = sb[me_m]
    ng[me_m] = sbn[me_m]

    for n in range(2):
        for direction in range(2):
            q = order[direction][n]
            y_copy(direction, q).wait_recv()
            y_far(direction, q).start()
            core_copy(3 if direction == 0 else 1, q).start()

    def wait_slots(km, carry):
        for copy in to_slots(km):
            copy.wait_recv()
        return carry

    lax.fori_loop(1, 8, wait_slots, 0)

    z_up, z_dn = wrap(z + 1, 8), wrap(z - 1, 8)

    def around(direction, step):
        sign = 1 if direction == 0 else -1
        o = wrap(z - sign * (step - 1), 8)
        target = dev(z_up if direction == 0 else z_dn, c, y)
        if step < 4:
            part = qg.at[o]
        else:
            part = qg.at[o, :, pl.ds(4 * direction, 4)]
        return remote(part, part, as_.at[direction, step - 1], ar.at[direction, step - 1], target)

    for direction in range(2):
        around(direction, 1).start()

    for n in range(2, 4):
        for direction in range(2):
            q = order[direction][n]
            y_copy(direction, q).wait_recv()
            core_copy(3 if direction == 0 else 1, q).start()

    def wait_small(k, carry):
        table_copy(k).wait_recv()
        match_copy(k).wait_recv()
        return carry

    lax.fori_loop(1, 8, wait_small, 0)
    to_smem = pltpu.make_async_copy(mmv, mms, loc.at[1])
    to_smem.start()

    def biases(d, carry):
        rows = tig[d].astype(jnp.float32)
        pages = rows[0:32]
        whole = rows[32:33]
        rest = rows[33:34]
        slot = lax.broadcasted_iota(jnp.int32, (32, 128), 0).astype(jnp.float32)
        before = (slot < whole).astype(jnp.float32)
        at = (slot == whole).astype(jnp.float32)
        within = lax.broadcasted_iota(jnp.int32, (PAGE, 128), 0).astype(jnp.float32) < rest
        for m in range(8):
            same = (pages == (z * 8 + m).astype(jnp.float32)).astype(jnp.float32)
            full = jnp.sum(same * before, axis=0, keepdims=True)
            more = full + jnp.sum(same * at, axis=0, keepdims=True)
            low = jnp.where(full > 0.0, jnp.log(jnp.maximum(full, 1.0)) * LOG2E, DEAD)
            high = jnp.where(more > 0.0, jnp.log(jnp.maximum(more, 1.0)) * LOG2E, DEAD)
            bi[d, m * PAGE : (m + 1) * PAGE, :] = jnp.where(within, high, low)
        return carry

    lax.fori_loop(0, 8, biases, 0)

    for step in (1, 2):
        for direction in range(2):
            around(direction, step).wait_recv()
            around(direction, step + 1).start()

    for q in range(4):
        y_far(0 if q < 2 else 1, q).wait_recv()
        core_copy(2, q).start()
    for dy in range(4):
        for q in range(4):
            core_copy(dy, q).wait_recv()
    own_pages.wait()
    to_smem.wait()

    eye = (
        lax.broadcasted_iota(jnp.int32, (128, 128), 0) == lax.broadcasted_iota(jnp.int32, (128, 128), 1)
    ).astype(jnp.float32).astype(jnp.bfloat16)

    def select_pages(d, carry):
        for pair in range(4):
            picks = [mms[2 * pair + k, 0, d * 8 + me_m] for k in range(2)]
            for h in range(2):
                values = []
                for k in range(2):
                    m = 2 * pair + k
                    kd[d, h, m * PAGE : (m + 1) * PAGE, :] = pgs[m, picks[k], 0, h]
                    values.append(pgs[m, picks[k], 1, h])
                turned = lax.dot_general(
                    eye, jnp.concatenate(values, axis=0), NT, preferred_element_type=jnp.float32
                )
                vt[d, h, :, pair * 128 : (pair + 1) * 128] = turned.astype(jnp.bfloat16)
        return carry

    lax.fori_loop(0, 8, select_pages, 0)

    def unit(o, d):
        h = o // 4
        q = qg[o, :, d].reshape(128, 128)
        s = lax.dot_general(kd[d, h], q, NT, preferred_element_type=jnp.float32)
        s = s * SCALE + bi[d]
        top = jnp.max(s, axis=0, keepdims=True)
        w = jnp.exp2(s - top)
        total = jnp.sum(w, axis=0, keepdims=True)
        acc = jnp.dot(vt[d, h], w.astype(jnp.bfloat16), preferred_element_type=jnp.float32)
        return acc, top, total

    row16 = lax.broadcasted_iota(jnp.int32, (16, 128), 0)

    def pack(direction, k, d, part):
        acc, top, total = part
        rs_out[direction, k, d, 0:128, :] = acc.astype(jnp.bfloat16)
        stats = jnp.zeros((16, 128), jnp.float32)
        for n, row in enumerate(split3(top) + split3(total)):
            stats = jnp.where(row16 == n, row, stats)
        rs_out[direction, k, d, 128:144, :] = stats.astype(jnp.bfloat16)

    def unpack(direction, k, d):
        acc = rs_in[direction, k, d, 0:128, :].astype(jnp.float32)
        st = rs_in[direction, k, d, 128:144, :].astype(jnp.float32)
        return acc, st[0:1] + st[1:2] + st[2:3], st[3:4] + st[4:5] + st[5:6]

    def back(direction, k, d):
        target = dev(z_dn if direction == 0 else z_up, c, y)
        return remote(
            rs_out.at[direction, k - 1, d], rs_in.at[direction, k - 1, d],
            rss.at[direction, k - 1, d], rsr.at[direction, k - 1, d], target,
        )

    for direction in range(2):
        around(direction, 3).wait_recv()
        around(direction, 4).start()
    for direction in range(2):
        around(direction, 4).wait_recv()

    far = lax.rem(z + 4, 8)

    for direction in range(2):
        def far_step(d, carry):
            pack(direction, 3, d, unit(far, d))
            back(direction, 4, d).start()
            return carry

        lax.fori_loop(4 * direction, 4 * direction + 4, far_step, 0)

    for k in (3, 2, 1):
        for direction in range(2):
            o = wrap(z - k if direction == 0 else z + k, 8)
            lo, hi = (4 * direction, 4 * direction + 4) if k == 3 else (0, 8)

            def with_in(d, carry):
                part = unit(o, d)
                back(direction, k + 1, d).wait_recv()
                pack(direction, k - 1, d, merge(part, unpack(direction, k, d)))
                back(direction, k, d).start()
                return carry

            def without(d, carry):
                pack(direction, k - 1, d, unit(o, d))
                back(direction, k, d).start()
                return carry

            lax.fori_loop(lo, hi, with_in, 0)
            if k == 3:
                lax.fori_loop(4 - lo, 8 - lo, without, 0)

    lane = lax.broadcasted_iota(jnp.int32, (64, 128), 1)
    nrow = lax.broadcasted_iota(jnp.int32, (64, 128), 0)

    def finish(d, carry):
        part = unit(z, d)
        q = qg[z, :, d].reshape(128, 128)
        keys = jnp.concatenate([ng[2 * u, d // 2] for u in range(4)], axis=0)
        vals = jnp.concatenate([ng[2 * u + 1, d // 2] for u in range(4)], axis=0)
        s = lax.dot_general(keys, q, NT, preferred_element_type=jnp.float32) * SCALE
        valid = (
            ((nrow // 8) % 2 == d % 2) & (nrow % 8 == lane % 8) & (nrow // 16 <= (lane // 8) % 4)
        )
        s = jnp.where(valid, s, DEAD)
        top = jnp.max(s, axis=0, keepdims=True)
        w = jnp.exp2(s - top)
        total = jnp.sum(w, axis=0, keepdims=True)
        turned = lax.dot_general(eye, vals, NT, preferred_element_type=jnp.float32).astype(jnp.bfloat16)
        acc = jnp.dot(turned, w.astype(jnp.bfloat16), preferred_element_type=jnp.float32)
        part = merge(part, (acc, top, total))
        for direction in range(2):
            back(direction, 1, d).wait_recv()
            part = merge(part, unpack(direction, 0, d))
        acc, _, total = part
        rows = jnp.transpose(acc / total).astype(jnp.bfloat16)
        for h in range(4):
            out[h, d] = rows[h * 32 : (h + 1) * 32]
        return carry

    lax.fori_loop(0, 8, finish, 0)

    def wait_spread_send(k, carry):
        spread(k // 8, k % 8).wait_send()
        return carry

    lax.fori_loop(1, 64, wait_spread_send, 0)

    def wait_small_send(k, carry):
        table_copy(k).wait_send()
        match_copy(k).wait_send()
        for copy in to_slots(k):
            copy.wait_send()
        return carry

    lax.fori_loop(1, 8, wait_small_send, 0)
    for q in range(4):
        for direction in range(2):
            y_copy(direction, q).wait_send()
        y_far(0 if q < 2 else 1, q).wait_send()
        for dy in range(4):
            core_copy(dy, q).wait_send()
    for direction in range(2):
        for step in range(1, 5):
            around(direction, step).wait_send()

        def wait_back(d, carry):
            for k in (1, 2, 3):
                back(direction, k, d).wait_send()
            return carry

        lax.fori_loop(0, 8, wait_back, 0)

        def wait_far(d, carry):
            back(direction, 4, d).wait_send()
            return carry

        lax.fori_loop(4 * direction, 4 * direction + 4, wait_far, 0)


def attend(qx, ti, mm, pages):
    bf, f32 = jnp.bfloat16, jnp.float32
    vm = pltpu.VMEM
    dma = pltpu.SemaphoreType.DMA
    return pl.pallas_call(
        attend_kernel,
        out_shape=jax.ShapeDtypeStruct((4, 8, 32, 128), bf),
        in_specs=[pl.BlockSpec(memory_space=pltpu.VMEM)] * 4,
        out_specs=pl.BlockSpec(memory_space=pltpu.VMEM),
        scratch_shapes=[
            vm((8, 8, 32, 128), bf),
            vm((8, 8, 16, 128), bf),
            vm((8, 4, 16, 128), bf),
            vm((8, 8, 8, 16, 128), bf),
            vm((8, 4, 16, 128), bf),
            vm((8, 48, 128), bf),
            vm((8, 1, 128), jnp.int32),
            pltpu.SMEM((8, 1, 128), jnp.int32),
            vm((8, 16, 2, 2, PAGE, 128), bf),
            vm((8, 2, 512, 128), bf),
            vm((8, 2, 128, 512), bf),
            vm((8, 512, 128), f32),
            vm((2, 4, 8, 144, 128), bf),
            vm((2, 4, 8, 144, 128), bf),
            dma((64,)), dma((64,)),
            dma((8,)), dma((8,)),
            dma((8,)), dma((8,)),
            dma((2,)),
            dma((2, 4)), dma((2, 4)),
            dma((4,)), dma((4,)),
            dma((4, 4)), dma((4, 4)),
            dma((8,)), dma((8,)),
            dma((8,)), dma((8,)),
            dma((2, 4)), dma((2, 4)),
            dma((2, 4, 8)), dma((2, 4, 8)),
        ],
        compiler_params=pltpu.CompilerParams(
            collective_id=1, has_side_effects=True, vmem_limit_bytes=48 * MIB
        ),
        name="attend",
    )(qx, ti, mm, pages)


def project_kernel(a, w_hbm, out, w, g, acc, xs, xr, wsem, zs, zr, cs, cr, xss, xsr):
    z, c, y = here()
    kx = lax.axis_index("kv")
    z_up, z_dn = wrap(z + 1, 8), wrap(z - 1, 8)
    w_copy = pltpu.make_async_copy(w_hbm, w, wsem.at[0])
    w_copy.start()
    bar = pltpu.get_barrier_semaphore()
    for target in (dev(z_up, c, y), dev(z_dn, c, y), dev(z, 1 - c, y)):
        pl.semaphore_signal(bar, inc=1, device_id=target, device_id_type=MESH)
    for dx in range(1, 4):
        pl.semaphore_signal(bar, inc=1, device_id={"kv": wrap(kx + dx, 4)}, device_id_type=MESH)
    ds = 8 // NG
    own = [pltpu.make_async_copy(a, g.at[c, z], wsem.at[1])]
    own[0].start()
    pl.semaphore_wait(bar, 6)

    def rows(ref, r):
        return ref.at[:, pl.ds(r * ds, ds)]

    def around(direction, step, r):
        sign = 1 if direction == 0 else -1
        o = wrap(z - sign * (step - 1), 8)
        target = dev(z_up if direction == 0 else z_dn, c, y)
        if step == 1:
            return remote(rows(a, r), rows(g.at[c, o], r), zs.at[direction, 0, r], zr.at[direction, 0, r], target)
        part = g.at[c, o]
        part = rows(part, r) if step < 4 else part.at[pl.ds(2 * direction, 2), pl.ds(r * ds, ds)]
        return remote(part, part, zs.at[direction, step - 1, r], zr.at[direction, step - 1, r], target)

    def across(dz, r):
        o = wrap(z + dz, 8)
        src = rows(a, r) if dz == 0 else rows(g.at[c, o], r)
        return remote(src, rows(g.at[c, o], r), cs.at[dz, r], cr.at[dz, r], dev(z, 1 - c, y))

    for r in range(NG):
        for direction in range(2):
            around(direction, 1, r).start()
        across(0, r).start()

    w_copy.wait()
    own[0].wait()

    def exchange(dx, r):
        return remote(
            xs.at[dx - 1, r], xr.at[dx - 1, r], xss.at[dx - 1, r], xsr.at[dx - 1, r], {"kv": wrap(kx + dx, 4)}
        )

    def use(o, r, first):
        o = wrap(o, 8)
        block = g[:, o, :, pl.ds(r * ds, ds)].reshape(2, 4, ds * 32, 128)
        left = jnp.concatenate(
            [jnp.concatenate([block[cc, h] for h in range(4)], axis=1) for cc in range(2)], axis=0
        )
        step = jnp.dot(
            left, w[pl.ds(pl.multiple_of(o * 512, 512), 512), :], preferred_element_type=jnp.float32
        )
        if first:
            acc[r] = step
        else:
            acc[r] += step

    def send_sums(r):
        for dx in range(1, 4):
            kk = wrap(kx + dx, 4)
            xs[dx - 1, r] = acc[r, :, pl.ds(pl.multiple_of(kk * 256, 256), 256)].astype(jnp.bfloat16)
            exchange(dx, r).start()

    def add_sums(r):
        total = acc[r, :, pl.ds(pl.multiple_of(kx * 256, 256), 256)]
        for dx in range(1, 4):
            exchange(dx, r).wait_recv()
            total = total + xr[dx - 1, r].astype(jnp.float32)
        out[:, pl.ds(r * ds, ds)] = total.astype(jnp.bfloat16).reshape(2, ds, 32, 256)

    for r in range(NG):
        across(0, r).wait_recv()
        use(z, r, True)
        for step in range(1, 4):
            for direction in range(2):
                sign = 1 if direction == 0 else -1
                around(direction, step, r).wait_recv()
                around(direction, step + 1, r).start()
                across((-sign * step) % 8, r).start()
            for direction in range(2):
                sign = 1 if direction == 0 else -1
                across((-sign * step) % 8, r).wait_recv()
                use(z - sign * step, r, False)
        for direction in range(2):
            around(direction, 4, r).wait_recv()
        across(4, r).start()
        across(4, r).wait_recv()
        use(z + 4, r, False)
        send_sums(r)
        if r > 0:
            add_sums(r - 1)
    add_sums(NG - 1)

    for r in range(NG):
        for direction in range(2):
            for step in range(1, 5):
                around(direction, step, r).wait_send()
        for dz in range(8):
            across(dz, r).wait_send()
        for dx in range(1, 4):
            exchange(dx, r).wait_send()


def project(a, w):
    bf, f32 = jnp.bfloat16, jnp.float32
    vm = pltpu.VMEM
    dma = pltpu.SemaphoreType.DMA
    rows_g = 512 // NG
    return pl.pallas_call(
        project_kernel,
        out_shape=jax.ShapeDtypeStruct((2, 8, 32, 256), bf),
        in_specs=[pl.BlockSpec(memory_space=pltpu.VMEM), pl.BlockSpec(memory_space=pl.ANY)],
        out_specs=pl.BlockSpec(memory_space=pltpu.VMEM),
        scratch_shapes=[
            vm((4096, 1024), bf),
            vm((2, 8, 4, 8, 32, 128), bf),
            vm((NG, rows_g, 1024), f32),
            vm((3, NG, rows_g, 256), bf),
            vm((3, NG, rows_g, 256), bf),
            dma((2,)),
            dma((2, 4, NG)), dma((2, 4, NG)),
            dma((8, NG)), dma((8, NG)),
            dma((3, NG)), dma((3, NG)),
        ],
        compiler_params=pltpu.CompilerParams(
            collective_id=2, has_side_effects=True, vmem_limit_bytes=48 * MIB
        ),
        name="project",
    )(a, w)


def body(prefill_kv, page_match, queries, new_kv, slot_request, page_table, context_len, out_weight):
    bf = jnp.bfloat16
    q = queries.reshape(8, 2, 2, 8, 4, HD).transpose(3, 4, 1, 2, 0, 5).reshape(8, 8, 16, HD)
    new = new_kv.transpose(3, 1, 2, 0, 4).reshape(2, 1, 8, 8, HD)
    new = jnp.broadcast_to(new, (2, 4, 8, 8, HD)).reshape(8, 8, 8, HD)
    request = slot_request.reshape(8, 1)
    ids = jnp.concatenate(
        [jnp.broadcast_to(request // 8, (8, 64)), jnp.broadcast_to(request % 8, (8, 64))], axis=1
    ).astype(bf)
    ids = jnp.broadcast_to(ids[None, None], (8, 8, 8, HD))
    qx = jnp.concatenate([q, new, ids], axis=2)
    lengths = context_len.reshape(1, 8)
    ti = jnp.concatenate(
        [page_table.reshape(8, MAXP).T, lengths // PAGE, lengths % PAGE, jnp.zeros((14, 8), jnp.int32)], axis=0
    )
    ti = jnp.tile(ti, (1, 16)).astype(bf)
    mm = jnp.pad(page_match.reshape(1, 64), ((0, 0), (0, 64)))
    a = attend(qx, ti, mm, prefill_kv)
    out = project(a, out_weight)
    out = out.reshape(2, 8, 4, 8, 256).transpose(1, 0, 3, 2, 4)
    return out.reshape(128, 1, STEPS, 256)


def solution(mesh):
    in_specs = (
        P(("pre", "grp"), None, "kv", None, None),
        P(("pre", "grp"), None, None),
        P(("pre", "grp"), None, "kv", None),
        P(("pre", "grp"), None, None, "kv", None),
        P("pre", "grp"),
        P("pre", "grp", None),
        P("pre", "grp"),
        P("kv", "pre"),
    )
    out_specs = P(None, "grp", None, ("pre", "kv"))
    return jax.shard_map(body, mesh=mesh, in_specs=in_specs, out_specs=out_specs, check_vma=False)
```

time: 329 us -> 179 us (0.54)
  waiting for transfers between devices: 218 us -> 0 us
  Pallas kernels: 0 us -> 171 us
  matrix products: 36.3 us -> 0 us
  local copies, waits for them, and re-layouts: 35.2 us -> 5.18 us
  starting transfers between devices: 13.7 us -> 0 us
  between operations: 13.3 us -> 0.05 us
  other arithmetic: 12.1 us -> 2.24 us
    pallas_call x0 -> x2, Pallas kernels: none -> 171 us  [the longest x1 108 us: attend(): pl.pallas_call(attend_kernel, out_shape=jax.ShapeDtypeStruct((4, 8, 32, 1...]
    all_gather x3 -> x0, waiting for transfers between devices: 159 us -> none  [the longest x1 72.6 us: body(): piece_new = lax.all_gather(flat_new, ('pre', 'grp'), axis=0, tiled=True)]
    dot_general x7 -> x0, matrix products: 36.3 us -> none  [the longest x1 10.6 us: body(): jnp.dot(shard_rows.reshape(-1, shard_rows.shape[-1]), out_weight, preferr...]
    reduce_scatter x1 -> x0, waiting for transfers between devices: 30.6 us -> none  [body(): lax.psum_scatter(partial_value, 'kv', scatter_dimension=3, tiled=True)]
    all_to_all x1 -> x0, waiting for transfers between devices: 28.5 us -> none  [body(): lax.all_to_all(sectioned, ('pre', 'grp'), split_axis=0, concat_axis=0, ti...]
    gather x2 -> x0, local copies, waits for them, and re-layouts: 15 us -> none  [the longest x1 12 us: body(): fetched = page_pool[tables]]
    slice x2 -> x0, local copies, waits for them, and re-layouts: 14.9 us -> none  [the longest x1 14.9 us: body(): fetched[:, :, 0]]
    all_to_all x1 -> x0, starting transfers between devices: 13.3 us -> none  [body(): lax.all_to_all(sectioned, ('pre', 'grp'), split_axis=0, concat_axis=0, ti...]
  transfers between devices with their start and end apart: 5 -> 0, of which waited for: 5 -> 0; matrix products, arithmetic and copies ran while one was open for 12% -> 0% of each run, Pallas kernels for 0% -> 0%
where the time goes in v1:
time: 179 us; the launch traced here: 178 us
  Pallas kernels  171 us (96%)
  local copies, waits for them, and re-layouts  5.18 us (3%)
  other arithmetic  2.24 us (1%)
    pallas_call x1, Pallas kernels, attend(): pl.pallas_call(attend_kernel, out_shape=jax.ShapeDtypeStruct((4, 8, 32, 1...  108 us
    pallas_call x1, Pallas kernels, project(): pl.pallas_call(project_kernel, out_shape=jax.ShapeDtypeStruct((2, 8, 32,...  62.8 us

profile of v1, /device:TPU:1, one launch (start us, length us, event | category | flops | bytes accessed | tf_op | source)
XLA Modules:
  0.0 178.3 jit_solution(6734970153829885671)
XLA Ops:
  0.0 0.7 convert_bitcast_fusion
  0.7 0.1 concatenate.19
  0.7 0.1 concatenate.20
  0.8 0.1 pad_maximum_fusion.1
  0.9 1.1 copy.15
  2.0 0.8 copy.16
  2.8 0.1 pad_maximum_fusion.qx
  2.9 0.7 fusion.3
  3.6 0.1 copy.17
  3.7 0.1 copy.18
  3.8 0.7 convert.23
  4.5 0.1 pad.8.clone
  4.6 0.1 maximum_maximum_fusion
  4.6 0.1 copy.19.ti
  4.7 0.7 pad.4.mm
  5.4 0.0 copy-start
  5.4 1.2 copy-done
  6.6 108.1 %attend.1.a = bf16[4,8,32,128]{3,2,1,0:T(8,128)(2,1)S(1)} custom-call(bf16[8,8,32,128]{3,2,1,0:T(8,128)(2,1)S(1)} %pad_maximum_fusion.qx, bf16[48,128]{1,0:T(8,128)(2,1)S(1)} %copy.19.ti, s32[1,128]{1,0:T(1,128)S(1)} %pad.4.mm, bf16[16,2,2,64,128]{4,3,2,1,0:T(8,128)(2,1)S(1)} %copy-done), custom_call_target="tpu_custom_call" | custom-call | tf_op jit(solution)/shard_map/attend/pallas_call | solution.py:433
  114.7 62.8 %project.1 = bf16[2,8,32,256]{3,2,1,0:T(8,128)(2,1)S(1)} custom-call(bf16[4,8,32,128]{3,2,1,0:T(8,128)(2,1)S(1)} %attend.1.a, bf16[4096,1024]{1,0:T(8,128)(2,1)} %w_hbm.1), custom_call_target="tpu_custom_call" | custom-call | tf_op jit(solution)/shard_map/project/pallas_call | solution.py:584
  177.5 0.8 copy.20
  (5 shorter events, 0.1 us)
Async XLA Ops:
  5.4 1.2 copy-start

commit v2 on v0

v2 whole, which is shorter than its diff:
```python
import functools

import jax
import jax.numpy as jnp
from jax import lax
from jax.experimental import pallas as pl
from jax.experimental.pallas import tpu as pltpu
from jax.sharding import PartitionSpec as P

MESH = pl.DeviceIdType.MESH
HD = 128
PAGE = 64
STEPS = 4
MAXP = 32
NZ = 8
NM = 8
LOG2E = 1.4426950408889634
SCALE = LOG2E / HD**0.5
DEAD = -float(2**100)
MIB = 1 << 20
NG = 4
GROUPS = ((0, 1), (1, 2), (3, 2), (5, 3))
PAIRS = (0, 3, 1, 2)
NT = (((1,), (1,)), ((), ()))


def here():
    p = lax.axis_index("pre")
    return p // 2, p % 2, lax.axis_index("grp")


def dev(z, c, y):
    return {"pre": z * 2 + c, "grp": y}


def dev_zm(z, m):
    return dev(z, m // 4, m % 4)


def wrap(a, n):
    return lax.rem(a + 2 * n, n)


def remote(src, dst, ssem, rsem, device):
    return pltpu.make_async_remote_copy(
        src_ref=src, dst_ref=dst, send_sem=ssem, recv_sem=rsem, device_id=device, device_id_type=MESH
    )


def rank(rel):
    return 0 if rel == 0 else 2 * rel - 1 if rel <= 4 else 2 * (8 - rel)


def merge(a, b):
    acc_a, m_a, l_a = a
    acc_b, m_b, l_b = b
    top = jnp.maximum(m_a, m_b)
    fa = jnp.exp2(m_a - top)
    fb = jnp.exp2(m_b - top)
    return acc_a * fa + acc_b * fb, top, l_a * fa + l_b * fb


def iota(shape, dim):
    return lax.broadcasted_iota(jnp.int32, shape, dim)


def one_hot(mask):
    return mask.astype(jnp.float32).astype(jnp.bfloat16)


def kernel(
    q_in, new_in, table_in, len_in, req_in, match_in, pg_hbm, w_hbm, out,
    qx, i1, qg, ng, nh, mmv, mms, pages0, pages1, pages2, pages3, kd, vt, bi, rs_out, rs_in, w, g, acc, xs, xr,
    loc, sps, spr, nhs, nhr, mss, msr, qys, qyr, qfs, qfr, qcs, qcr, ys, yr, ys2, yr2, cs, cr, as_, ar, rss, rsr,
    zs, zr, ks, kr, xss, xsr,
):
    z, c, y = here()
    kx = lax.axis_index("kv")
    me_m = c * 4 + y
    z_up, z_dn = wrap(z + 1, 8), wrap(z - 1, 8)
    y_up, y_dn = wrap(y + 1, 4), wrap(y - 1, 4)

    bar = pltpu.get_barrier_semaphore()
    for k in range(1, 8):
        pl.semaphore_signal(bar, inc=1, device_id=dev(wrap(z + k, 8), c, y), device_id_type=MESH)
        pl.semaphore_signal(bar, inc=1, device_id=dev_zm(z, wrap(me_m + k, 8)), device_id_type=MESH)
    for dx in range(1, 4):
        pl.semaphore_signal(bar, inc=1, device_id={"kv": wrap(kx + dx, 4)}, device_id_type=MESH)
    pages_at = (pages0, pages1, pages2, pages3)
    own_pages = pltpu.make_async_copy(pg_hbm, pages0.at[c], loc.at[0])
    own_pages.start()
    w_copy = pltpu.make_async_copy(w_hbm, w, loc.at[2])
    w_copy.start()

    row = iota((128, 1024), 0)
    origin = (row % 8) * 128 + ((row // 8) % 4) * 32 + row // 32 - iota((128, 1024), 1)

    def arrange(zj, carry):
        hot = one_hot(origin == -4 * zj)
        rows = jnp.dot(hot, q_in[...].reshape(1024, 128), preferred_element_type=jnp.float32)
        qx[zj, 0:8] = rows.astype(jnp.bfloat16).reshape(8, 16, 128)
        return carry

    lax.fori_loop(0, 8, arrange, 0)
    row = iota((128, 128), 0)
    lane = iota((128, 128), 1)
    origin = (row % 8) * 16 + ((row // 8) % 4) * 4 + ((row // 32) % 2) * 2 + row // 64
    new = jnp.dot(one_hot(origin == lane), new_in[...], preferred_element_type=jnp.float32).astype(jnp.bfloat16)
    lane8 = iota((8, 128), 1)
    facts = jnp.concatenate([table_in[...], jnp.zeros((8, 128 - MAXP), jnp.int32)], axis=1)

    def to_column(ref):
        line = jnp.concatenate([ref[...], jnp.zeros((1, 120), jnp.int32)], axis=1)
        line = jnp.where(lane8 == iota((8, 128), 0), jnp.broadcast_to(line, (8, 128)), 0)
        return jnp.broadcast_to(jnp.sum(line, axis=1, keepdims=True), (8, 128))

    length = to_column(len_in)
    request = to_column(req_in)
    for n, values in enumerate((length >> 6, length & 63, request >> 3, request & 7)):
        facts = jnp.where(lane8 == MAXP + n, values, facts)
    facts = facts.astype(jnp.float32)
    facts = jnp.concatenate([facts, facts], axis=0).astype(jnp.bfloat16)
    for zj in range(8):
        qx[zj, 8] = new[16 * zj : 16 * zj + 16]
        qx[zj, 9] = facts
    i1[me_m, 0] = qx[z]
    mmv[me_m] = jnp.concatenate([match_in[...], jnp.zeros((1, 64), jnp.int32)], axis=1)
    pl.semaphore_wait(bar, 17)

    def spread(kz):
        zj = wrap(z + kz, 8)
        return remote(qx.at[zj], i1.at[me_m, rank(8 - kz)], sps.at[kz], spr.at[rank(8 - kz)], dev(zj, c, y))

    def match_copy(km):
        return remote(mmv.at[me_m], mmv.at[me_m], mss.at[km], msr.at[km], dev_zm(z, wrap(me_m + km, 8)))

    def m_of(cc, yy):
        return cc * 4 + wrap(yy, 4)

    def y_dev(direction):
        return dev(z, c, y_up if direction == 0 else y_dn)

    def m_behind(direction):
        return m_of(c, y - 1 if direction == 0 else y + 1)

    def part(m, gi, tile, tiles):
        lo, n = GROUPS[gi]
        return i1.at[m, pl.ds(lo, n), pl.ds(tile, tiles)]

    def q_y(direction, gi):
        ref = part(me_m, gi, 0, 9)
        return remote(ref, ref, qys.at[direction, gi], qyr.at[direction, gi], y_dev(direction))

    def q_far(direction, gi):
        ref = part(m_behind(direction), gi, 5 * direction, 5 - direction)
        return remote(ref, ref, qfs.at[direction, gi], qfr.at[direction, gi], y_dev(direction))

    def q_core(dy, gi):
        ref = part(m_of(c, y + dy), gi, 0, 9)
        return remote(ref, ref, qcs.at[dy, gi], qcr.at[dy, gi], dev(z, 1 - c, y))

    behind = (3, 1)

    def quarter(dy, q):
        return pages_at[dy].at[c, pl.ds(4 * q, 4)]

    def y_copy(direction, q):
        return remote(
            quarter(0, q), quarter(behind[direction], q), ys.at[direction, q], yr.at[direction, q], y_dev(direction)
        )

    def y_far(direction, q):
        return remote(quarter(behind[direction], q), quarter(2, q), ys2.at[q], yr2.at[q], y_dev(direction))

    def core_copy(dy, q):
        return remote(quarter(dy, q), quarter(dy, q), cs.at[dy, q], cr.at[dy, q], dev(z, 1 - c, y))

    order = ((0, 1, 2, 3), (2, 3, 0, 1))

    for kz in (1, 7, 2, 6, 3, 5, 4):
        spread(kz).start()
    for km in range(1, 8):
        match_copy(km).start()

    def send_group(gi):
        q_y(0, gi).start()
        q_y(1, gi).start()
        q_core(0, gi).start()

    def send_pages(n):
        for direction in range(2):
            y_copy(direction, order[direction][n]).start()

    def forward_pages(n):
        for direction in range(2):
            q = order[direction][n]
            y_copy(direction, q).wait_recv()
            if n < 2:
                y_far(direction, q).start()
            core_copy(behind[direction], q).start()

    send_group(0)
    own_pages.wait()
    send_pages(0)
    for gi in range(1, 4):
        lo, n = GROUPS[gi]
        for rk in range(lo, lo + n):
            kz = [k for k in range(1, 8) if rank(8 - k) == rk][0]
            spread(kz).wait_recv()
        send_group(gi)
    for gi in range(4):
        for direction in range(2):
            q_y(direction, gi).wait_recv()
            q_far(direction, gi).start()
            q_core(behind[direction], gi).start()
    send_pages(1)
    forward_pages(0)
    send_pages(2)
    send_pages(3)
    for q in range(4):
        core_copy(0, q).start()

    def biases(d, carry):
        rows = i1[me_m, from_plane(d), 9].astype(jnp.float32)
        rows = jnp.transpose(jnp.concatenate([rows] * 8, axis=0))
        pages = rows[0:32]
        whole = rows[32:33]
        rest = rows[33:34]
        slot = iota((32, 128), 0).astype(jnp.float32)
        before = (slot < whole).astype(jnp.float32)
        at = (slot == whole).astype(jnp.float32)
        within = iota((PAGE, 128), 0).astype(jnp.float32) < rest
        for m in range(8):
            number = z * 8 + m_of(m % 2, y + PAIRS[m // 2])
            same = (pages == number.astype(jnp.float32)).astype(jnp.float32)
            full = jnp.sum(same * before, axis=0, keepdims=True)
            more = full + jnp.sum(same * at, axis=0, keepdims=True)
            low = jnp.where(full > 0.0, jnp.log(jnp.maximum(full, 1.0)) * LOG2E, DEAD)
            high = jnp.where(more > 0.0, jnp.log(jnp.maximum(more, 1.0)) * LOG2E, DEAD)
            bi[d, m * PAGE : (m + 1) * PAGE, :] = jnp.where(within, high, low)
        return carry

    def from_plane(d):
        rel = wrap(d - z, 8)
        return jnp.where(rel == 0, 0, jnp.where(rel <= 4, 2 * rel - 1, 2 * (8 - rel)))

    for gi in range(4):
        for direction in range(2):
            q_far(direction, gi).wait_recv()
        q_core(2, gi).start()
    for gi in range(4):
        for dy in (0, 1, 3, 2):
            q_core(dy, gi).wait_recv()

    facts = jnp.concatenate([i1[me_m, from_plane(d), 9] for d in range(8)], axis=0).astype(jnp.float32)
    source = facts[:, 34:35].astype(jnp.int32)
    within = facts[:, 35:36].astype(jnp.int32)
    rel = ((source >> 3) - z + 8) & 7
    ranked = jnp.where(rel == 0, 0, jnp.where(rel <= 4, 2 * rel - 1, 2 * (8 - rel)))
    column = ((source & 7) * 8 + ranked) * 16 + within
    column = jnp.broadcast_to(column, (128, 1024)) + (iota((128, 1024), 0) & 8)
    hot = one_hot(column == iota((128, 1024), 1))
    for fp in range(9):
        rows = jnp.dot(
            hot, i1[:, :, fp].reshape(1024, 128), preferred_element_type=jnp.float32
        ).astype(jnp.bfloat16).reshape(8, 16, 128)
        if fp < 8:
            qg[z, fp] = rows
        else:
            ng[...] = rows

    def around(direction, step):
        sign = 1 if direction == 0 else -1
        o = wrap(z - sign * (step - 1), 8)
        ref = qg.at[o] if step < 4 else qg.at[o, :, pl.ds(4 * direction, 4)]
        target = dev(z_up if direction == 0 else z_dn, c, y)
        return remote(ref, ref, as_.at[direction, step - 1], ar.at[direction, step - 1], target)

    def pass_on(step):
        for direction in range(2):
            around(direction, step).wait_recv()
            around(direction, step + 1).start()

    for direction in range(2):
        around(direction, 1).start()

    def new_copy(kz):
        zj = wrap(z + kz, 8)
        return remote(ng.at[zj], nh.at[z], nhs.at[kz], nhr.at[kz], dev(zj, c, y))

    for kz in range(1, 8):
        new_copy(kz).start()
    nh[z] = ng[z]

    lax.fori_loop(0, 8, biases, 0)
    eye = one_hot(row == lane)

    def select_pages(pair):
        dy = PAIRS[pair]

        def one(d, carry):
            picks = [mms[m_of(k, y + dy), 0, d * 8 + me_m] for k in range(2)]
            for h in range(2):
                values = []
                for k in range(2):
                    m = 2 * pair + k
                    kd[d, h, m * PAGE : (m + 1) * PAGE, :] = pages_at[dy][k, picks[k], 0, h]
                    values.append(pages_at[dy][k, picks[k], 1, h])
                turned = lax.dot_general(
                    eye, jnp.concatenate(values, axis=0), NT, preferred_element_type=jnp.float32
                )
                vt[d, h, :, pair * 128 : (pair + 1) * 128] = turned.astype(jnp.bfloat16)
            return carry

        lax.fori_loop(0, 8, one, 0)

    def wait_cores(dy):
        for q in range(4):
            core_copy(dy, q).wait_recv()

    for km in range(1, 8):
        match_copy(km).wait_recv()
    to_smem = pltpu.make_async_copy(mmv, mms, loc.at[1])
    to_smem.start()
    forward_pages(1)
    to_smem.wait()
    wait_cores(0)
    select_pages(0)
    pass_on(1)
    forward_pages(2)
    pass_on(2)
    forward_pages(3)
    wait_cores(3)
    select_pages(1)
    wait_cores(1)
    select_pages(2)
    pass_on(3)
    for q in range(4):
        y_far(0 if q < 2 else 1, q).wait_recv()
        core_copy(2, q).start()
    wait_cores(2)
    select_pages(3)
    for direction in range(2):
        around(direction, 4).wait_recv()
    for kz in range(1, 8):
        new_copy(kz).wait_recv()

    def unit(o, d):
        h = o // 4
        q = qg[o, :, d].reshape(128, 128)
        s = lax.dot_general(kd[d, h], q, NT, preferred_element_type=jnp.float32)
        s = s * SCALE + bi[d]
        top = jnp.max(s, axis=0, keepdims=True)
        wt = jnp.exp2(s - top)
        total = jnp.sum(wt, axis=0, keepdims=True)
        part = jnp.dot(vt[d, h], wt.astype(jnp.bfloat16), preferred_element_type=jnp.float32)
        return part, top, total

    nrow = iota((32, 128), 0)
    nlane = iota((32, 128), 1)
    valid = (nrow % 8 == nlane % 8) & (nrow // 8 <= (nlane // 8) % 4)

    def fresh(o):
        h = o // 4
        q = qg[o, :, z].reshape(128, 128)
        keys = nh[pl.ds(4 * h, 2)].reshape(32, 128)
        vals = nh[pl.ds(4 * h + 2, 2)].reshape(32, 128)
        s = lax.dot_general(keys, q, NT, preferred_element_type=jnp.float32) * SCALE
        s = jnp.where(valid, s, DEAD)
        top = jnp.max(s, axis=0, keepdims=True)
        wt = jnp.exp2(s - top)
        total = jnp.sum(wt, axis=0, keepdims=True)
        turned = lax.dot_general(eye, vals, NT, preferred_element_type=jnp.float32).astype(jnp.bfloat16)
        part = jnp.dot(turned, wt.astype(jnp.bfloat16), preferred_element_type=jnp.float32)
        return part, top, total

    def units(o, half):
        num, top, total = fresh(o)
        return [
            merge(unit(o, d), (num, jnp.where(z == d, top, DEAD), total)) for d in range(4 * half, 4 * half + 4)
        ]

    row16 = iota((16, 128), 0)

    def back(direction, k, half):
        target = dev(z_dn if direction == 0 else z_up, c, y)
        return remote(
            rs_out.at[direction, k - 1, half], rs_in.at[direction, k - 1, half],
            rss.at[direction, k - 1, half], rsr.at[direction, k - 1, half], target,
        )

    def unpack(direction, k, half):
        st = rs_in[direction, k - 1, half, 512:528, :].astype(jnp.float32)
        return [
            (
                rs_in[direction, k - 1, half, 128 * i : 128 * i + 128, :].astype(jnp.float32),
                st[3 * i : 3 * i + 1],
                st[3 * i + 1 : 3 * i + 2] + st[3 * i + 2 : 3 * i + 3],
            )
            for i in range(4)
        ]

    def give(direction, k, half, o, merged):
        parts = units(o, half)
        if merged:
            back(direction, k + 1, half).wait_recv()
            parts = [merge(a, b) for a, b in zip(parts, unpack(direction, k + 1, half))]
        stats = jnp.zeros((16, 128), jnp.float32)
        for i, (num, top, total) in enumerate(parts):
            top_b = top.astype(jnp.bfloat16).astype(jnp.float32)
            shift = jnp.exp2(top - top_b)
            top, total = top_b, total * shift
            rs_out[direction, k - 1, half, 128 * i : 128 * i + 128, :] = (num * shift).astype(jnp.bfloat16)
            total_hi = total.astype(jnp.bfloat16).astype(jnp.float32)
            for n, values in enumerate((top, total_hi, total - total_hi)):
                stats = jnp.where(row16 == 3 * i + n, values, stats)
        rs_out[direction, k - 1, half, 512:528, :] = stats.astype(jnp.bfloat16)
        back(direction, k, half).start()

    for direction in range(2):
        give(direction, 4, direction, wrap(z + 4, 8), False)
    for k in (3, 2, 1):
        for n in range(2):
            for direction in range(2):
                half = direction if n == 0 else 1 - direction
                give(direction, k, half, wrap(z - k if direction == 0 else z + k, 8), k < 3 or n == 0)

    ds = 8 // NG

    def rows_of(ref, r):
        return ref.at[:, pl.ds(r * ds, ds)]

    def gather(direction, step, r):
        sign = 1 if direction == 0 else -1
        o = wrap(z - sign * (step - 1), 8)
        ref = g.at[c, o]
        ref = rows_of(ref, r) if step < 4 else ref.at[pl.ds(2 * direction, 2), pl.ds(r * ds, ds)]
        target = dev(z_up if direction == 0 else z_dn, c, y)
        return remote(ref, ref, zs.at[direction, step - 1, r], zr.at[direction, step - 1, r], target)

    def across(dz, r):
        ref = rows_of(g.at[c, wrap(z + dz, 8)], r)
        return remote(ref, ref, ks.at[dz, r], kr.at[dz, r], dev(z, 1 - c, y))

    parts = units(z, 0) + units(z, 1)
    for half in range(2):
        for direction in range(2):
            back(direction, 1, half).wait_recv()
        below, above = unpack(0, 1, half), unpack(1, 1, half)
        for i in range(4):
            d = 4 * half + i
            num, _, total = merge(merge(parts[d], below[i]), above[i])
            rows = jnp.transpose(num / total).astype(jnp.bfloat16)
            for h in range(4):
                g[c, z, h, d] = rows[h * 32 : (h + 1) * 32]
            if (d + 1) % ds == 0:
                r = d // ds
                for direction in range(2):
                    gather(direction, 1, r).start()
                across(0, r).start()

    w_copy.wait()

    def exchange(dx, r):
        return remote(
            xs.at[dx - 1, r], xr.at[dx - 1, r], xss.at[dx - 1, r], xsr.at[dx - 1, r], {"kv": wrap(kx + dx, 4)}
        )

    def use(o, r, first):
        o = wrap(o, 8)
        block = g[:, o, :, pl.ds(r * ds, ds)].reshape(2, 4, ds * 32, 128)
        left = jnp.concatenate(
            [jnp.concatenate([block[cc, h] for h in range(4)], axis=1) for cc in range(2)], axis=0
        )
        step = jnp.dot(
            left, w[pl.ds(pl.multiple_of(o * 512, 512), 512), :], preferred_element_type=jnp.float32
        )
        if first:
            acc[r] = step
        else:
            acc[r] += step

    def send_sums(r):
        for dx in range(1, 4):
            kk = wrap(kx + dx, 4)
            xs[dx - 1, r] = acc[r, :, pl.ds(pl.multiple_of(kk * 256, 256), 256)].astype(jnp.bfloat16)
            exchange(dx, r).start()

    def add_sums(r):
        total = acc[r, :, pl.ds(pl.multiple_of(kx * 256, 256), 256)]
        for dx in range(1, 4):
            exchange(dx, r).wait_recv()
            total = total + xr[dx - 1, r].astype(jnp.float32)
        out[:, pl.ds(r * ds, ds)] = total.astype(jnp.bfloat16).reshape(2, ds, 32, 256)

    for r in range(NG):
        across(0, r).wait_recv()
        use(z, r, True)
    waiting = []

    def settle(left):
        while len(waiting) > left:
            dz, r = waiting.pop(0)
            across(dz % 8, r).wait_recv()
            use(z + dz, r, False)
            if dz == 4:
                send_sums(r)
                if r > 0:
                    add_sums(r - 1)

    for step in range(1, 4):
        for r in range(NG):
            for direction in range(2):
                dz = -step if direction == 0 else step
                gather(direction, step, r).wait_recv()
                gather(direction, step + 1, r).start()
                across(dz % 8, r).start()
                waiting.append((dz, r))
            settle(2)
    for r in range(NG):
        for direction in range(2):
            gather(direction, 4, r).wait_recv()
        across(4, r).start()
        waiting.append((4, r))
        settle(1)
    settle(0)
    add_sums(NG - 1)

    for k in range(1, 8):
        spread(k).wait_send()
        match_copy(k).wait_send()
        new_copy(k).wait_send()
    for n in range(4):
        for direction in range(2):
            q_y(direction, n).wait_send()
            q_far(direction, n).wait_send()
            y_copy(direction, n).wait_send()
        y_far(0 if n < 2 else 1, n).wait_send()
        for dy in range(4):
            q_core(dy, n).wait_send()
            core_copy(dy, n).wait_send()
    for direction in range(2):
        for step in range(1, 5):
            around(direction, step).wait_send()
        for k in (1, 2, 3):
            for half in range(2):
                back(direction, k, half).wait_send()
        back(direction, 4, direction).wait_send()
    for r in range(NG):
        for direction in range(2):
            for step in range(1, 5):
                gather(direction, step, r).wait_send()
        for dz in range(8):
            across(dz, r).wait_send()
        for dx in range(1, 4):
            exchange(dx, r).wait_send()


def decode(*args):
    bf, f32 = jnp.bfloat16, jnp.float32
    vm = pltpu.VMEM
    dma = pltpu.SemaphoreType.DMA
    rows_g = 512 // NG
    return pl.pallas_call(
        kernel,
        out_shape=jax.ShapeDtypeStruct((2, 8, 32, 256), bf),
        in_specs=[pl.BlockSpec(memory_space=pltpu.VMEM)] * 6 + [pl.BlockSpec(memory_space=pl.ANY)] * 2,
        out_specs=pl.BlockSpec(memory_space=pltpu.VMEM),
        scratch_shapes=[
            vm((8, 10, 16, 128), bf),
            vm((8, 8, 10, 16, 128), bf),
            vm((8, 8, 8, 16, 128), bf),
            vm((8, 16, 128), bf),
            vm((8, 16, 128), bf),
            vm((8, 1, 128), jnp.int32),
            pltpu.SMEM((8, 1, 128), jnp.int32),
            vm((2, 16, 2, 2, PAGE, 128), bf),
            vm((2, 16, 2, 2, PAGE, 128), bf),
            vm((2, 16, 2, 2, PAGE, 128), bf),
            vm((2, 16, 2, 2, PAGE, 128), bf),
            vm((8, 2, 512, 128), bf),
            vm((8, 2, 128, 512), bf),
            vm((8, 512, 128), f32),
            vm((2, 4, 2, 528, 128), bf),
            vm((2, 4, 2, 528, 128), bf),
            vm((4096, 1024), bf),
            vm((2, 8, 4, 8, 32, 128), bf),
            vm((NG, rows_g, 1024), f32),
            vm((3, NG, rows_g, 256), bf),
            vm((3, NG, rows_g, 256), bf),
            dma((3,)),
            dma((8,)), dma((8,)),
            dma((8,)), dma((8,)),
            dma((8,)), dma((8,)),
            dma((2, 4)), dma((2, 4)),
            dma((2, 4)), dma((2, 4)),
            dma((4, 4)), dma((4, 4)),
            dma((2, 4)), dma((2, 4)),
            dma((4,)), dma((4,)),
            dma((4, 4)), dma((4, 4)),
            dma((2, 4)), dma((2, 4)),
            dma((2, 4, 2)), dma((2, 4, 2)),
            dma((2, 4, NG)), dma((2, 4, NG)),
            dma((8, NG)), dma((8, NG)),
            dma((3, NG)), dma((3, NG)),
        ],
        compiler_params=pltpu.CompilerParams(
            collective_id=1, has_side_effects=True, vmem_limit_bytes=60 * MIB
        ),
        name="decode",
    )(*args)


def body(prefill_kv, page_match, queries, new_kv, slot_request, page_table, context_len, out_weight):
    out = decode(
        queries, new_kv.reshape(128, HD), page_table.reshape(8, MAXP), context_len.reshape(1, 8),
        slot_request.reshape(1, 8), page_match.reshape(1, 64), prefill_kv, out_weight,
    )
    out = out.reshape(2, 8, 4, 8, 256).transpose(1, 0, 3, 2, 4)
    return out.reshape(128, 1, STEPS, 256)


def solution(mesh):
    in_specs = (
        P(("pre", "grp"), None, "kv", None, None),
        P(("pre", "grp"), None, None),
        P(("pre", "grp"), None, "kv", None),
        P(("pre", "grp"), None, None, "kv", None),
        P("pre", "grp"),
        P("pre", "grp", None),
        P("pre", "grp"),
        P("kv", "pre"),
    )
    out_specs = P(None, "grp", None, ("pre", "kv"))
    return jax.shard_map(body, mesh=mesh, in_specs=in_specs, out_specs=out_specs, check_vma=False)
```

time: 329 us -> 129 us (0.39)
  waiting for transfers between devices: 218 us -> 0 us
  Pallas kernels: 0 us -> 126 us
  matrix products: 36.3 us -> 0 us
  local copies, waits for them, and re-layouts: 35.2 us -> 1.78 us
  starting transfers between devices: 13.7 us -> 0 us
  between operations: 13.3 us -> 0.01 us
  other arithmetic: 12.1 us -> 0 us
    all_gather x3 -> x0, waiting for transfers between devices: 159 us -> none  [the longest x1 72.6 us: body(): piece_new = lax.all_gather(flat_new, ('pre', 'grp'), axis=0, tiled=True)]
    pallas_call x0 -> x1, Pallas kernels: none -> 126 us  [decode(): pl.pallas_call(kernel, out_shape=jax.ShapeDtypeStruct((2, 8, 32, 256), bf...]
    dot_general x7 -> x0, matrix products: 36.3 us -> none  [the longest x1 10.6 us: body(): jnp.dot(shard_rows.reshape(-1, shard_rows.shape[-1]), out_weight, preferr...]
    reduce_scatter x1 -> x0, waiting for transfers between devices: 30.6 us -> none  [body(): lax.psum_scatter(partial_value, 'kv', scatter_dimension=3, tiled=True)]
    all_to_all x1 -> x0, waiting for transfers between devices: 28.5 us -> none  [body(): lax.all_to_all(sectioned, ('pre', 'grp'), split_axis=0, concat_axis=0, ti...]
    gather x2 -> x0, local copies, waits for them, and re-layouts: 15 us -> none  [the longest x1 12 us: body(): fetched = page_pool[tables]]
    slice x2 -> x0, local copies, waits for them, and re-layouts: 14.9 us -> none  [the longest x1 14.9 us: body(): fetched[:, :, 0]]
    all_to_all x1 -> x0, starting transfers between devices: 13.3 us -> none  [body(): lax.all_to_all(sectioned, ('pre', 'grp'), split_axis=0, concat_axis=0, ti...]
  transfers between devices with their start and end apart: 5 -> 0, of which waited for: 5 -> 0; matrix products, arithmetic and copies ran while one was open for 12% -> 0% of each run, Pallas kernels for 0% -> 0%
where the time goes in v2:
time: 129 us; the launch traced here: 128 us
  Pallas kernels  126 us (98%)
  local copies, waits for them, and re-layouts  1.78 us (1%)
    pallas_call x1, Pallas kernels, decode(): pl.pallas_call(kernel, out_shape=jax.ShapeDtypeStruct((2, 8, 32, 256), bf...  126 us

profile of v2, /device:TPU:1, one launch (start us, length us, event | category | flops | bytes accessed | tf_op | source)
XLA Modules:
  0.0 128.3 jit_solution(13666316778100725494)
XLA Ops:
  0.0 126.5 %decode.1 = bf16[2,8,32,256]{3,2,1,0:T(8,128)(2,1)} custom-call(bf16[8,4,32,128]{3,2,1,0:T(8,128)(2,1)} %q_in.1, bf16[128,128]{1,0:T(8,128)(2,1)} %bitcast.10, s32[8,32]{1,0:T(8,128)} %bitcast.11, s32[1,8]{1,0:T(1,128)} %bitcast.12, s32[1,8]{1,0:T(1,128)} %bitcast.13, s32[1,64]{1,0:T(1,128)} %bitcast.14, bf16[16,2,2,64,128]{4,3,2,1,0:T(8,128)(2,1)} %pg_hbm.1, ...), custom_call_target="tpu_custom_call" | custom-call | tf_op jit(solution)/shard_map/decode/pallas_call | solution.py:564
  126.5 1.8 %copy.9 = bf16[8,2,8,4,256]{4,3,2,1,0:T(4,128)(2,1)} copy(bf16[8,2,8,4,256]{4,2,3,0,1:T(8,128)(2,1)} %bitcast.9) | data formatting | bytes 524288 | tf_op jit(solution)/shard_map/transpose | solution.py:619

commit v3 on v2

--- a/solution.py
+++ b/solution.py
@@ -19,8 +19,9 @@
 DEAD = -float(2**100)
 MIB = 1 << 20
 NG = 4
-GROUPS = ((0, 1), (1, 2), (3, 2), (5, 3))
+GROUPS = ((0, 2), (2, 2), (4, 2), (6, 2))
 PAIRS = (0, 3, 1, 2)
+CHUNKS = (((0, 2), (2, 4), (6, 2), (8, 8)), ((8, 2), (10, 4), (14, 2), (0, 8)))
 NT = (((1,), (1,)), ((), ()))
 
 
@@ -48,7 +49,7 @@
 
 
 def rank(rel):
-    return 0 if rel == 0 else 2 * rel - 1 if rel <= 4 else 2 * (8 - rel)
+    return 0 if rel == 0 else 1 if rel == 4 else 8 - 2 * rel if rel < 4 else 2 * rel - 7
 
 
 def merge(a, b):
@@ -60,6 +61,11 @@
     return acc_a * fa + acc_b * fb, top, l_a * fa + l_b * fb
 
 
+def ranks(rel):
+    side = jnp.where(rel < 4, 8 - 2 * rel, 2 * rel - 7)
+    return jnp.where(rel == 0, 0, jnp.where(rel == 4, 1, side))
+
+
 def iota(shape, dim):
     return lax.broadcasted_iota(jnp.int32, shape, dim)
 
@@ -69,8 +75,9 @@
 
 
 def kernel(
-    q_in, new_in, table_in, len_in, req_in, match_in, pg_hbm, w_hbm, out,
-    qx, i1, qg, ng, nh, mmv, mms, pages0, pages1, pages2, pages3, kd, vt, bi, rs_out, rs_in, w, g, acc, xs, xr,
+    q_hbm, new_hbm, table_hbm, len_hbm, req_hbm, match_hbm, pg_hbm, w_hbm, out,
+    q_in, new_in, table_in, len_in, req_in, match_in,
+    qf, qx, i1, qg, ng, nh, mmv, mms, pages0, pages1, pages2, pages3, kd, vt, bi, rs_out, rs_in, w, g, acc, xs, xr,
     loc, sps, spr, nhs, nhr, mss, msr, qys, qyr, qfs, qfr, qcs, qcr, ys, yr, ys2, yr2, cs, cr, as_, ar, rss, rsr,
     zs, zr, ks, kr, xss, xsr,
 ):
@@ -80,6 +87,17 @@
     z_up, z_dn = wrap(z + 1, 8), wrap(z - 1, 8)
     y_up, y_dn = wrap(y + 1, 4), wrap(y - 1, 4)
 
+    loads = [
+        pltpu.make_async_copy(src, dst, loc.at[3 + n])
+        for n, (src, dst) in enumerate(
+            (
+                (q_hbm, q_in), (new_hbm, new_in), (table_hbm, table_in), (len_hbm, len_in), (req_hbm, req_in),
+                (match_hbm, match_in),
+            )
+        )
+    ]
+    for load in loads:
+        load.start()
     bar = pltpu.get_barrier_semaphore()
     for k in range(1, 8):
         pl.semaphore_signal(bar, inc=1, device_id=dev(wrap(z + k, 8), c, y), device_id_type=MESH)
@@ -92,13 +110,15 @@
     w_copy = pltpu.make_async_copy(w_hbm, w, loc.at[2])
     w_copy.start()
 
-    row = iota((128, 1024), 0)
-    origin = (row % 8) * 128 + ((row // 8) % 4) * 32 + row // 32 - iota((128, 1024), 1)
+    for load in loads:
+        load.wait()
+    qf[...] = q_in[...].reshape(1024, 128).astype(jnp.float32)
 
     def arrange(zj, carry):
-        hot = one_hot(origin == -4 * zj)
-        rows = jnp.dot(hot, q_in[...].reshape(1024, 128), preferred_element_type=jnp.float32)
-        qx[zj, 0:8] = rows.astype(jnp.bfloat16).reshape(8, 16, 128)
+        for tile in range(8):
+            h, t = tile // 2, 2 * (tile % 2)
+            rows = [qf[pl.ds((t + k) * 32 + 4 * zj + h, 8, stride=128), :] for k in range(2)]
+            qx[zj, tile] = jnp.concatenate(rows, axis=0).astype(jnp.bfloat16)
         return carry
 
     lax.fori_loop(0, 8, arrange, 0)
@@ -161,23 +181,28 @@
 
     behind = (3, 1)
 
-    def quarter(dy, q):
-        return pages_at[dy].at[c, pl.ds(4 * q, 4)]
-
-    def y_copy(direction, q):
+    def chunk(dy, lo, n):
+        return pages_at[dy].at[c, pl.ds(lo, n)]
+
+    def y_copy(direction, n):
+        lo, count = CHUNKS[direction][n]
         return remote(
-            quarter(0, q), quarter(behind[direction], q), ys.at[direction, q], yr.at[direction, q], y_dev(direction)
+            chunk(0, lo, count), chunk(behind[direction], lo, count),
+            ys.at[direction, n], yr.at[direction, n], y_dev(direction),
         )
 
-    def y_far(direction, q):
-        return remote(quarter(behind[direction], q), quarter(2, q), ys2.at[q], yr2.at[q], y_dev(direction))
-
-    def core_copy(dy, q):
-        return remote(quarter(dy, q), quarter(dy, q), cs.at[dy, q], cr.at[dy, q], dev(z, 1 - c, y))
-
-    order = ((0, 1, 2, 3), (2, 3, 0, 1))
-
-    for kz in (1, 7, 2, 6, 3, 5, 4):
+    def y_far(direction, n):
+        lo, count = CHUNKS[direction][n]
+        return remote(
+            chunk(behind[direction], lo, count), chunk(2, lo, count),
+            ys2.at[direction, n], yr2.at[direction, n], y_dev(direction),
+        )
+
+    def core_copy(dy, n):
+        lo, count = ((CHUNKS[0][:3] + CHUNKS[1][:3]) if dy == 2 else CHUNKS[1 if dy == 1 else 0])[n]
+        return remote(chunk(dy, lo, count), chunk(dy, lo, count), cs.at[dy, n], cr.at[dy, n], dev(z, 1 - c, y))
+
+    for kz in (4, 3, 5, 2, 6, 1, 7):
         spread(kz).start()
     for km in range(1, 8):
         match_copy(km).start()
@@ -189,36 +214,34 @@
 
     def send_pages(n):
         for direction in range(2):
-            y_copy(direction, order[direction][n]).start()
+            y_copy(direction, n).start()
 
     def forward_pages(n):
         for direction in range(2):
-            q = order[direction][n]
-            y_copy(direction, q).wait_recv()
-            if n < 2:
-                y_far(direction, q).start()
-            core_copy(behind[direction], q).start()
-
-    send_group(0)
+            y_copy(direction, n).wait_recv()
+            if n < 3:
+                y_far(direction, n).start()
+            core_copy(behind[direction], n).start()
+
     own_pages.wait()
     send_pages(0)
-    for gi in range(1, 4):
+    for gi in range(4):
         lo, n = GROUPS[gi]
-        for rk in range(lo, lo + n):
+        for rk in range(max(lo, 1), lo + n):
             kz = [k for k in range(1, 8) if rank(8 - k) == rk][0]
             spread(kz).wait_recv()
         send_group(gi)
+    send_pages(1)
     for gi in range(4):
         for direction in range(2):
             q_y(direction, gi).wait_recv()
             q_far(direction, gi).start()
             q_core(behind[direction], gi).start()
-    send_pages(1)
     forward_pages(0)
     send_pages(2)
     send_pages(3)
-    for q in range(4):
-        core_copy(0, q).start()
+    for n in range(4):
+        core_copy(0, n).start()
 
     def biases(d, carry):
         rows = i1[me_m, from_plane(d), 9].astype(jnp.float32)
@@ -242,7 +265,7 @@
 
     def from_plane(d):
         rel = wrap(d - z, 8)
-        return jnp.where(rel == 0, 0, jnp.where(rel <= 4, 2 * rel - 1, 2 * (8 - rel)))
+        return ranks(rel)
 
     for gi in range(4):
         for direction in range(2):
@@ -256,7 +279,7 @@
     source = facts[:, 34:35].astype(jnp.int32)
     within = facts[:, 35:36].astype(jnp.int32)
     rel = ((source >> 3) - z + 8) & 7
-    ranked = jnp.where(rel == 0, 0, jnp.where(rel <= 4, 2 * rel - 1, 2 * (8 - rel)))
+    ranked = ranks(rel)
     column = ((source & 7) * 8 + ranked) * 16 + within
     column = jnp.broadcast_to(column, (128, 1024)) + (iota((128, 1024), 0) & 8)
     hot = one_hot(column == iota((128, 1024), 1))
@@ -315,8 +338,8 @@
         lax.fori_loop(0, 8, one, 0)
 
     def wait_cores(dy):
-        for q in range(4):
-            core_copy(dy, q).wait_recv()
+        for n in range(6 if dy == 2 else 4):
+            core_copy(dy, n).wait_recv()
 
     for km in range(1, 8):
         match_copy(km).wait_recv()
@@ -335,9 +358,10 @@
     wait_cores(1)
     select_pages(2)
     pass_on(3)
-    for q in range(4):
-        y_far(0 if q < 2 else 1, q).wait_recv()
-        core_copy(2, q).start()
+    for n in range(3):
+        for direction in range(2):
+            y_far(direction, n).wait_recv()
+            core_copy(2, 3 * direction + n).start()
     wait_cores(2)
     select_pages(3)
     for direction in range(2):
@@ -422,8 +446,8 @@
     for k in (3, 2, 1):
         for n in range(2):
             for direction in range(2):
-                half = direction if n == 0 else 1 - direction
-                give(direction, k, half, wrap(z - k if direction == 0 else z + k, 8), k < 3 or n == 0)
+                half = 1 - direction if n == 0 else direction
+                give(direction, k, half, wrap(z - k if direction == 0 else z + k, 8), k < 3 or n == 1)
 
     ds = 8 // NG
 
@@ -441,6 +465,10 @@
     def across(dz, r):
         ref = rows_of(g.at[c, wrap(z + dz, 8)], r)
         return remote(ref, ref, ks.at[dz, r], kr.at[dz, r], dev(z, 1 - c, y))
+
+    def start_gather(r):
+        for direction in range(2):
+            gather(direction, 1, r).start()
 
     parts = units(z, 0) + units(z, 1)
     for half in range(2):
@@ -455,9 +483,33 @@
                 g[c, z, h, d] = rows[h * 32 : (h + 1) * 32]
             if (d + 1) % ds == 0:
                 r = d // ds
-                for direction in range(2):
-                    gather(direction, 1, r).start()
+                if r < 2:
+                    start_gather(r)
                 across(0, r).start()
+
+    for k in range(1, 8):
+        spread(k).wait_send()
+        match_copy(k).wait_send()
+        new_copy(k).wait_send()
+    for n in range(4):
+        for direction in range(2):
+            q_y(direction, n).wait_send()
+            q_far(direction, n).wait_send()
+            y_copy(direction, n).wait_send()
+        for dy in range(4):
+            q_core(dy, n).wait_send()
+            if dy != 2:
+                core_copy(dy, n).wait_send()
+    for n in range(6):
+        y_far(n // 3, n % 3).wait_send()
+        core_copy(2, n).wait_send()
+    for direction in range(2):
+        for step in range(1, 5):
+            around(direction, step).wait_send()
+        for k in (1, 2, 3):
+            for half in range(2):
+                back(direction, k, half).wait_send()
+        back(direction, 4, direction).wait_send()
 
     w_copy.wait()
 
@@ -508,44 +560,24 @@
                 if r > 0:
                     add_sums(r - 1)
 
-    for step in range(1, 4):
-        for r in range(NG):
+    for slot in range(1, 4 + NG):
+        if 2 <= slot + 1 < NG:
+            start_gather(slot + 1)
+        for r in reversed(range(NG)):
+            step = slot - r
+            if not 1 <= step <= 4:
+                continue
             for direction in range(2):
-                dz = -step if direction == 0 else step
                 gather(direction, step, r).wait_recv()
-                gather(direction, step + 1, r).start()
+                if step < 4:
+                    gather(direction, step + 1, r).start()
+            for dz in (-step, step) if step < 4 else (4,):
                 across(dz % 8, r).start()
                 waiting.append((dz, r))
-            settle(2)
-    for r in range(NG):
-        for direction in range(2):
-            gather(direction, 4, r).wait_recv()
-        across(4, r).start()
-        waiting.append((4, r))
-        settle(1)
+            settle(4 if step < 4 else 1)
     settle(0)
     add_sums(NG - 1)
 
-    for k in range(1, 8):
-        spread(k).wait_send()
-        match_copy(k).wait_send()
-        new_copy(k).wait_send()
-    for n in range(4):
-        for direction in range(2):
-            q_y(direction, n).wait_send()
-            q_far(direction, n).wait_send()
-            y_copy(direction, n).wait_send()
-        y_far(0 if n < 2 else 1, n).wait_send()
-        for dy in range(4):
-            q_core(dy, n).wait_send()
-            core_copy(dy, n).wait_send()
-    for direction in range(2):
-        for step in range(1, 5):
-            around(direction, step).wait_send()
-        for k in (1, 2, 3):
-            for half in range(2):
-                back(direction, k, half).wait_send()
-        back(direction, 4, direction).wait_send()
     for r in range(NG):
         for direction in range(2):
             for step in range(1, 5):
@@ -564,9 +596,16 @@
     return pl.pallas_call(
         kernel,
         out_shape=jax.ShapeDtypeStruct((2, 8, 32, 256), bf),
-        in_specs=[pl.BlockSpec(memory_space=pltpu.VMEM)] * 6 + [pl.BlockSpec(memory_space=pl.ANY)] * 2,
+        in_specs=[pl.BlockSpec(memory_space=pltpu.HBM)] * 8,
         out_specs=pl.BlockSpec(memory_space=pltpu.VMEM),
         scratch_shapes=[
+            vm((8, 4, 32, 128), bf),
+            vm((128, 128), bf),
+            vm((8, 32), jnp.int32),
+            vm((1, 8), jnp.int32),
+            vm((1, 8), jnp.int32),
+            vm((1, 64), jnp.int32),
+            vm((1024, 128), f32),
             vm((8, 10, 16, 128), bf),
             vm((8, 8, 10, 16, 128), bf),
             vm((8, 8, 8, 16, 128), bf),
@@ -588,7 +627,7 @@
             vm((NG, rows_g, 1024), f32),
             vm((3, NG, rows_g, 256), bf),
             vm((3, NG, rows_g, 256), bf),
-            dma((3,)),
+            dma((9,)),
             dma((8,)), dma((8,)),
             dma((8,)), dma((8,)),
             dma((8,)), dma((8,)),
@@ -596,8 +635,8 @@
             dma((2, 4)), dma((2, 4)),
             dma((4, 4)), dma((4, 4)),
             dma((2, 4)), dma((2, 4)),
-            dma((4,)), dma((4,)),
-            dma((4, 4)), dma((4, 4)),
+            dma((2, 3)), dma((2, 3)),
+            dma((4, 6)), dma((4, 6)),
             dma((2, 4)), dma((2, 4)),
             dma((2, 4, 2)), dma((2, 4, 2)),
             dma((2, 4, NG)), dma((2, 4, NG)),

time: 129 us -> 127 us (0.984)
  no operation moved by 1% of the time
where the time goes in v3:
time: 127 us
  Pallas kernels  125 us (98%)
  local copies, waits for them, and re-layouts  1.78 us (1%)
    pallas_call x1, Pallas kernels, decode(): pl.pallas_call(kernel, out_shape=jax.ShapeDtypeStruct((2, 8, 32, 256), bf...  125 us

profile of v3, /device:TPU:1, one launch (start us, length us, event | category | flops | bytes accessed | tf_op | source)
XLA Modules:
  0.0 127.2 jit_solution(4772933647325687534)
XLA Ops:
  0.0 125.4 %decode.1 = bf16[2,8,32,256]{3,2,1,0:T(8,128)(2,1)} custom-call(bf16[8,4,32,128]{3,2,1,0:T(8,128)(2,1)} %q_hbm.1, bf16[128,128]{1,0:T(8,128)(2,1)} %bitcast.10, s32[8,32]{1,0:T(8,128)} %bitcast.11, s32[1,8]{1,0:T(1,128)} %bitcast.12, s32[1,8]{1,0:T(1,128)} %bitcast.13, s32[1,64]{1,0:T(1,128)} %bitcast.14, bf16[16,2,2,64,128]{4,3,2,1,0:T(8,128)(2,1)} %pg_hbm.1, ...), custom_call_target="tpu_custom_call" | custom-call | tf_op jit(solution)/shard_map/decode/pallas_call | solution.py:596
  125.4 1.8 %copy.9 = bf16[8,2,8,4,256]{4,3,2,1,0:T(4,128)(2,1)} copy(bf16[8,2,8,4,256]{4,2,3,0,1:T(8,128)(2,1)} %bitcast.9) | data formatting | bytes 524288 | tf_op jit(solution)/shard_map/transpose | solution.py:658

commit v4 on v3

--- a/solution.py
+++ b/solution.py
@@ -112,7 +112,7 @@
 
     for load in loads:
         load.wait()
-    qf[...] = q_in[...].reshape(1024, 128).astype(jnp.float32)
+    qf[0:1024, :] = q_in[...].reshape(1024, 128).astype(jnp.float32)
 
     def arrange(zj, carry):
         for tile in range(8):
@@ -471,6 +471,26 @@
             gather(direction, 1, r).start()
 
     parts = units(z, 0) + units(z, 1)
+    for k in range(1, 8):
+        spread(k).wait_send()
+        match_copy(k).wait_send()
+        new_copy(k).wait_send()
+    for n in range(4):
+        for direction in range(2):
+            q_y(direction, n).wait_send()
+            q_far(direction, n).wait_send()
+            y_copy(direction, n).wait_send()
+        for dy in range(4):
+            q_core(dy, n).wait_send()
+            if dy != 2:
+                core_copy(dy, n).wait_send()
+    for n in range(6):
+        y_far(n // 3, n % 3).wait_send()
+        core_copy(2, n).wait_send()
+    for direction in range(2):
+        for step in range(1, 5):
+            around(direction, step).wait_send()
+
     for half in range(2):
         for direction in range(2):
             back(direction, 1, half).wait_recv()
@@ -487,30 +507,6 @@
                     start_gather(r)
                 across(0, r).start()
 
-    for k in range(1, 8):
-        spread(k).wait_send()
-        match_copy(k).wait_send()
-        new_copy(k).wait_send()
-    for n in range(4):
-        for direction in range(2):
-            q_y(direction, n).wait_send()
-            q_far(direction, n).wait_send()
-            y_copy(direction, n).wait_send()
-        for dy in range(4):
-            q_core(dy, n).wait_send()
-            if dy != 2:
-                core_copy(dy, n).wait_send()
-    for n in range(6):
-        y_far(n // 3, n % 3).wait_send()
-        core_copy(2, n).wait_send()
-    for direction in range(2):
-        for step in range(1, 5):
-            around(direction, step).wait_send()
-        for k in (1, 2, 3):
-            for half in range(2):
-                back(direction, k, half).wait_send()
-        back(direction, 4, direction).wait_send()
-
     w_copy.wait()
 
     def exchange(dx, r):
@@ -545,16 +541,13 @@
             total = total + xr[dx - 1, r].astype(jnp.float32)
         out[:, pl.ds(r * ds, ds)] = total.astype(jnp.bfloat16).reshape(2, ds, 32, 256)
 
-    for r in range(NG):
-        across(0, r).wait_recv()
-        use(z, r, True)
-    waiting = []
+    waiting = [(0, r) for r in range(NG)]
 
     def settle(left):
         while len(waiting) > left:
             dz, r = waiting.pop(0)
             across(dz % 8, r).wait_recv()
-            use(z + dz, r, False)
+            use(z + dz, r, dz == 0)
             if dz == 4:
                 send_sums(r)
                 if r > 0:
@@ -576,14 +569,19 @@
                 waiting.append((dz, r))
             settle(4 if step < 4 else 1)
     settle(0)
-    add_sums(NG - 1)
-
+    for direction in range(2):
+        for k in (1, 2, 3):
+            for half in range(2):
+                back(direction, k, half).wait_send()
+        back(direction, 4, direction).wait_send()
     for r in range(NG):
         for direction in range(2):
             for step in range(1, 5):
                 gather(direction, step, r).wait_send()
         for dz in range(8):
             across(dz, r).wait_send()
+    add_sums(NG - 1)
+    for r in range(NG):
         for dx in range(1, 4):
             exchange(dx, r).wait_send()
 
@@ -605,7 +603,7 @@
             vm((1, 8), jnp.int32),
             vm((1, 8), jnp.int32),
             vm((1, 64), jnp.int32),
-            vm((1024, 128), f32),
+            vm((1152, 128), f32),
             vm((8, 10, 16, 128), bf),
             vm((8, 8, 10, 16, 128), bf),
             vm((8, 8, 8, 16, 128), bf),

time: 127 us -> 127 us (level)
  no operation moved by 1% of the time
where the time goes in v4:
time: 127 us
  Pallas kernels  125 us (98%)
  local copies, waits for them, and re-layouts  1.78 us (1%)
    pallas_call x1, Pallas kernels, decode(): pl.pallas_call(kernel, out_shape=jax.ShapeDtypeStruct((2, 8, 32, 256), bf...  125 us

profile of v4, /device:TPU:1, one launch (start us, length us, event | category | flops | bytes accessed | tf_op | source)
XLA Modules:
  0.0 126.8 jit_solution(8596276604347416628)
XLA Ops:
  0.0 125.0 %decode.1 = bf16[2,8,32,256]{3,2,1,0:T(8,128)(2,1)} custom-call(bf16[8,4,32,128]{3,2,1,0:T(8,128)(2,1)} %q_hbm.1, bf16[128,128]{1,0:T(8,128)(2,1)} %bitcast.10, s32[8,32]{1,0:T(8,128)} %bitcast.11, s32[1,8]{1,0:T(1,128)} %bitcast.12, s32[1,8]{1,0:T(1,128)} %bitcast.13, s32[1,64]{1,0:T(1,128)} %bitcast.14, bf16[16,2,2,64,128]{4,3,2,1,0:T(8,128)(2,1)} %pg_hbm.1, ...), custom_call_target="tpu_custom_call" | custom-call | tf_op jit(solution)/shard_map/decode/pallas_call | solution.py:594
  125.1 1.8 %copy.9 = bf16[8,2,8,4,256]{4,3,2,1,0:T(4,128)(2,1)} copy(bf16[8,2,8,4,256]{4,2,3,0,1:T(8,128)(2,1)} %bitcast.9) | data formatting | bytes 524288 | tf_op jit(solution)/shard_map/transpose | solution.py:656
